TPU v7x, 256 devices: a whole 4x4x8 slice. The times are simulated.
256 devices in a mesh: gx: 8 (over z), gy: 8 (over x, core), gz: 4 (over y).
Axes of the slice: x: 4, y: 4, z: 8, core: 2. Of those that a mesh axis runs over, the one named last changes fastest.
Arguments:
- thermal_state: float32 [32, 256, 1024], P('gz', 'gy', 'gx'), may hold values from -6 to 6
- diffusion_ratio: float32 [32, 256, 1024], P('gz', 'gy', 'gx'), may hold values from 100 to 100000
Outputs:
- advanced: float32 [32, 256, 1024], P('gz', 'gy', 'gx')
All inputs are finite; a program needn't handle non-finite values.
Results may differ from a plain program's by a relative error of at most 0.0028.
Values sent between devices are 32-bit elements; how exact they have to be, the bound alone decides.
A program may use at most 64 MiB of HBM per device.

v0:
```python
import jax
import jax.numpy as jnp
from jax import lax
from jax.sharding import PartitionSpec as P


def extended(array, sides, width):
    for axis, dim in sides:
        peers, length = (lax.axis_size(axis), array.shape[dim])
        up = [(i, (i + 1) % peers) for i in range(peers - 1)]
        down = [(j, i) for i, j in up]
        last = lax.slice_in_dim(array, length - width, length, axis=dim)
        leading = lax.slice_in_dim(array, 0, width, axis=dim)
        before = lax.ppermute(last, axis, up)
        after = lax.ppermute(leading, axis, down)
        array = jnp.concatenate([before, array, after], axis=dim)
    return array


def shifted(value, axis, steps):
    count = lax.axis_size(axis)
    leading, last = (max(0, -steps), min(count, count - steps))
    return lax.ppermute(value, axis, [(source, source + steps) for source in range(leading, last)])


def earlier(values, stride, axis_dim, filler):
    length = values.shape[axis_dim]
    head_part = jnp.full_like(lax.slice_in_dim(values, 0, stride, axis=axis_dim), filler)
    return jnp.concatenate(
        [head_part, lax.slice_in_dim(values, 0, length - stride, axis=axis_dim)], axis=axis_dim
    )


def later(values, stride, axis_dim, filler):
    length = values.shape[axis_dim]
    tail_part = jnp.full_like(
        lax.slice_in_dim(values, length - stride, length, axis=axis_dim), filler
    )
    return jnp.concatenate(
        [lax.slice_in_dim(values, stride, length, axis=axis_dim), tail_part], axis=axis_dim
    )


def local_solve(lower_band, middle, upper_band, right_sides, axis_dim):
    length = middle.shape[axis_dim]
    stride = 1
    while stride < length:
        factor_low = lower_band / earlier(middle, stride, axis_dim, 1.0)
        factor_high = upper_band / later(middle, stride, axis_dim, 1.0)
        middle = (
            middle
            - factor_low * earlier(upper_band, stride, axis_dim, 0.0)
            - factor_high * later(lower_band, stride, axis_dim, 0.0)
        )
        right_sides = tuple(
            (
                side
                - factor_low * earlier(side, stride, axis_dim, 0.0)
                - factor_high * later(side, stride, axis_dim, 0.0)
                for side in right_sides
            )
        )
        lower_band = -factor_low * earlier(lower_band, stride, axis_dim, 0.0)
        upper_band = -factor_high * later(upper_band, stride, axis_dim, 0.0)
        stride = stride * 2
    return tuple((side / middle for side in right_sides))


def matmul_two(left_mat, right_mat):
    return (
        left_mat[0] * right_mat[0] + left_mat[1] * right_mat[2],
        left_mat[0] * right_mat[1] + left_mat[1] * right_mat[3],
        left_mat[2] * right_mat[0] + left_mat[3] * right_mat[2],
        left_mat[2] * right_mat[1] + left_mat[3] * right_mat[3],
    )


def apply_two(matrix, vector):
    return (
        matrix[0] * vector[0] + matrix[1] * vector[1],
        matrix[2] * vector[0] + matrix[3] * vector[1],
    )


def invert_two(matrix):
    determinant = matrix[0] * matrix[3] - matrix[1] * matrix[2]
    return (
        matrix[3] / determinant,
        -matrix[1] / determinant,
        -matrix[2] / determinant,
        matrix[0] / determinant,
    )


def split_system(system):
    return (
        (system[0], system[1], system[2], system[3]),
        (system[4], system[5], system[6], system[7]),
        (system[8], system[9]),
    )


def block_step(system, below, above):
    couple_low, couple_high, values = split_system(system)
    below_low, below_high, below_values = split_system(below)
    above_low, above_high, above_values = split_system(above)
    left_term = matmul_two(couple_low, below_high)
    right_term = matmul_two(couple_high, above_low)
    pivot = (
        1.0 - left_term[0] - right_term[0],
        -left_term[1] - right_term[1],
        -left_term[2] - right_term[2],
        1.0 - left_term[3] - right_term[3],
    )
    pivot_inverse = invert_two(pivot)
    new_low = matmul_two(pivot_inverse, matmul_two(couple_low, below_low))
    new_high = matmul_two(pivot_inverse, matmul_two(couple_high, above_high))
    from_low = apply_two(couple_low, below_values)
    from_high = apply_two(couple_high, above_values)
    new_values = apply_two(
        pivot_inverse,
        (values[0] - from_low[0] - from_high[0], values[1] - from_low[1] - from_high[1]),
    )
    return jnp.stack(
        [-entry for entry in new_low] + [-entry for entry in new_high] + list(new_values)
    )


def solve_gathered(whole):
    count = whole.shape[1]
    stride = 1
    while stride < count:
        whole = block_step(whole, earlier(whole, stride, 1, 0.0), later(whole, stride, 1, 0.0))
        stride = stride * 2
    return whole


def reduced_system(lower_band, middle, upper_band, right_side, solved, axis_dim):
    length = middle.shape[axis_dim]

    def row_of(values, index_at):
        return lax.index_in_dim(values, index_at, axis_dim, keepdims=False).reshape(-1)

    second = min(1, length - 1)
    before_last = max(length - 2, 0)
    base_part, first_resp, last_resp = solved
    low_first = row_of(lower_band, 0)
    up_first = row_of(upper_band, 0)
    low_last = row_of(lower_band, length - 1)
    up_last = row_of(upper_band, length - 1)
    diag_block = (
        row_of(middle, 0) + up_first * row_of(first_resp, second),
        up_first * row_of(last_resp, second),
        low_last * row_of(first_resp, before_last),
        row_of(middle, length - 1) + low_last * row_of(last_resp, before_last),
    )
    block_inverse = invert_two(diag_block)
    source_first = row_of(right_side, 0) - up_first * row_of(base_part, second)
    source_last = row_of(right_side, length - 1) - low_last * row_of(base_part, before_last)
    zero_line = jnp.zeros_like(low_first)
    couple_low = (zero_line, block_inverse[0] * low_first, zero_line, block_inverse[2] * low_first)
    couple_high = (block_inverse[1] * up_last, zero_line, block_inverse[3] * up_last, zero_line)
    values = apply_two(block_inverse, (source_first, source_last))
    return jnp.stack(list(couple_low) + list(couple_high) + list(values))


def line_solve(right_side, h_low, h_high, first_wall, last_wall, axis_dim, finish):
    length = right_side.shape[axis_dim]
    position = lax.broadcasted_iota(jnp.int32, right_side.shape, axis_dim)
    lower_band = jnp.where(first_wall, 0.0, -0.5 * h_low)
    upper_band = jnp.where(last_wall, 0.0, -0.5 * h_high)
    middle = 1.0 + 0.5 * (h_low + h_high)
    edge_rows = (position == 0) | (position == length - 1)
    sources = (
        jnp.where(edge_rows, 0.0, right_side),
        (position == 0).astype(right_side.dtype),
        (position == length - 1).astype(right_side.dtype),
    )
    solved = local_solve(
        jnp.where(edge_rows, 0.0, lower_band),
        jnp.where(edge_rows, 1.0, middle),
        jnp.where(edge_rows, 0.0, upper_band),
        sources,
        axis_dim,
    )
    system = reduced_system(lower_band, middle, upper_band, right_side, solved, axis_dim)
    first_value, last_value = finish(system)
    rest_shape = list(right_side.shape)
    rest_shape[axis_dim] = 1
    return (
        solved[0]
        + first_value.reshape(rest_shape) * solved[1]
        + last_value.reshape(rest_shape) * solved[2]
    )


def offset_slice(padded_field, axis_dim, shift_by):
    index_list = [slice(1, -1), slice(1, -1), slice(1, -1)]
    index_list[axis_dim] = slice(1 + shift_by, padded_field.shape[axis_dim] - 1 + shift_by)
    return padded_field[tuple(index_list)]


def directional(padded, axis_dim, place, count):
    field = offset_slice(padded[0], axis_dim, 0)
    cond_here = offset_slice(padded[1], axis_dim, 0)
    cond_low = offset_slice(padded[1], axis_dim, -1)
    cond_high = offset_slice(padded[1], axis_dim, 1)
    length = field.shape[axis_dim]
    position = lax.broadcasted_iota(jnp.int32, field.shape, axis_dim)
    first_wall = (position == 0) & (place == 0)
    last_wall = (position == length - 1) & (place == count - 1)
    h_low = jnp.where(
        first_wall, 2.0 * cond_here, 2.0 * cond_low * cond_here / (cond_low + cond_here)
    )
    h_high = jnp.where(
        last_wall, 2.0 * cond_here, 2.0 * cond_here * cond_high / (cond_here + cond_high)
    )
    laplace = h_low * (offset_slice(padded[0], axis_dim, -1) - field) + h_high * (
        offset_slice(padded[0], axis_dim, 1) - field
    )
    return (laplace, h_low, h_high, first_wall, last_wall)


def on_device(thermal_state, diffusion_ratio):
    sheet_bundle = jnp.stack([thermal_state, diffusion_ratio])
    padded = extended(sheet_bundle, (("gx", 3), ("gy", 2), ("gz", 1)), 1)
    implicit_depth_pass = directional(padded, 0, lax.axis_index("gz"), lax.axis_size("gz"))
    implicit_north_pass = directional(padded, 1, lax.axis_index("gy"), lax.axis_size("gy"))
    implicit_east_pass = directional(padded, 2, lax.axis_index("gx"), lax.axis_size("gx"))

    def finish_x(system):
        for bit_level in range(lax.axis_size("gx").bit_length() - 1):
            stride = 1 << bit_level
            below = shifted(system, "gx", stride)
            above = shifted(system, "gx", -stride)
            system = block_step(system, below, above)
        return (system[8], system[9])

    def finish_y(system):
        whole = solve_gathered(lax.all_gather(system[:, None], "gy", axis=1, tiled=True))
        own_part = lax.dynamic_index_in_dim(whole, lax.axis_index("gy"), 1, keepdims=False)
        return (own_part[8], own_part[9])

    def finish_z(system):
        whole = solve_gathered(lax.all_gather(system[:, None], "gz", axis=1, tiled=True))
        own_part = lax.dynamic_index_in_dim(whole, lax.axis_index("gz"), 1, keepdims=False)
        return (own_part[8], own_part[9])

    explicit_forcing = (
        thermal_state
        + 0.5 * implicit_east_pass[0]
        + implicit_north_pass[0]
        + implicit_depth_pass[0]
    )
    section_x = line_solve(
        explicit_forcing,
        implicit_east_pass[1],
        implicit_east_pass[2],
        implicit_east_pass[3],
        implicit_east_pass[4],
        2,
        finish_x,
    )
    section_y = line_solve(
        section_x - 0.5 * implicit_north_pass[0],
        implicit_north_pass[1],
        implicit_north_pass[2],
        implicit_north_pass[3],
        implicit_north_pass[4],
        1,
        finish_y,
    )
    return line_solve(
        section_y - 0.5 * implicit_depth_pass[0],
        implicit_depth_pass[1],
        implicit_depth_pass[2],
        implicit_depth_pass[3],
        implicit_depth_pass[4],
        0,
        finish_z,
    )


def solution(mesh):
    in_specs = (P("gz", "gy", "gx"), P("gz", "gy", "gx"))
    out_specs = P("gz", "gy", "gx")
    return jax.shard_map(
        on_device, mesh=mesh, in_specs=in_specs, out_specs=out_specs, check_vma=False
    )
```

profile of v0, /device:TPU:1, one launch (start us, length us, event | category | flops | bytes accessed | tf_op | source)
XLA Modules:
  0.0 191.4 jit_solution(5299207764395666750)
XLA Ops:
  1.2 1.3 collective-permute-start.1
  2.5 5.0 %collective-permute-start = (f32[2,8,32,1]{3,2,1,0:T(8,128)S(1)}, f32[2,8,32,1]{3,2,1,0:T(8,128)S(1)}, u32[]{:S(2)}, u32[]{:S(2)}) collective-permute-start(f32[2,8,32,1]{3,2,1,0:T(8,128)S(1)} %get-tuple-element.562), channel_id=1, source_target_pairs={{0,32},{32,64},{64,96},{96,128},{128,160},{160,192},{192,224},{1,3... | collective-permute-start | bytes 6152 | tf_op jit(solution)/shard_map/ppermute | solution.py:14
  12.1 6.2 %collective-permute-start.2 = (f32[2,8,1,130]{3,1,2,0:T(8,128)S(1)}, f32[2,8,1,130]{3,1,2,0:T(8,128)S(1)}, u32[]{:S(2)}, u32[]{:S(2)}) collective-permute-start(f32[2,8,1,130]{3,1,2,0:T(8,128)S(1)} %copy.222), channel_id=1, source_target_pairs={{0,4},{4,8},{8,12},{12,16},{16,20},{20,24},{24,28},{1,5},{5,9},{9,... | collective-permute-start | bytes 24968 | tf_op jit(solution)/shard_map/ppermute | solution.py:14
  18.9 1.9 collective-permute-start.3
  21.1 2.8 %collective-permute-done.3 = f32[2,8,1,130]{3,1,2,0:T(8,128)S(1)} collective-permute-done((f32[2,8,1,130]{3,1,2,0:T(8,128)S(1)}, f32[2,8,1,130]{3,1,2,0:T(8,128)S(1)}, u32[]{:S(2)}, u32[]{:S(2)}) %collective-permute-start.3) | collective-permute-done | bytes 8352 | tf_op jit(solution)/shard_map/ppermute | solution.py:15
  24.0 1.3 collective-permute-start.5
  25.3 4.0 %collective-permute-start.4 = (f32[2,1,34,130]{3,1,2,0:T(1,128)S(1)}, f32[2,1,34,130]{3,1,2,0:T(1,128)S(1)}, u32[]{:S(2)}, u32[]{:S(2)}) collective-permute-start(f32[2,1,34,130]{3,1,2,0:T(1,128)S(1)} %get-tuple-element.451), channel_id=1, source_target_pairs={{0,1},{1,2},{2,3},{4,5},{5,6},{6,7},{8,9},{9,10},{10,11},{12,13},{... | collective-permute-start | bytes 106088 | tf_op jit(solution)/shard_map/ppermute | solution.py:14
  31.8 1.2 broadcast_select_fusion.11
  42.2 1.3 collective-permute-start.7
  43.5 4.7 %collective-permute-start.6 = (f32[10,256]{1,0:T(8,128)S(1)}, f32[10,256]{1,0:T(8,128)S(1)}, u32[]{:S(2)}, u32[]{:S(2)}) collective-permute-start(f32[10,256]{1,0:T(8,128)S(1)} %stack.29), channel_id=1, source_target_pairs={{0,32},{32,64},{64,96},{96,128},{128,160},{160,192},{192,224},{1,3... | collective-permute-start | bytes 30728 | tf_op jit(solution)/shard_map/ppermute | solution.py:23
  54.4 1.3 collective-permute-start.9
  55.7 6.8 %collective-permute-start.8 = (f32[10,256]{1,0:T(8,128)}, f32[10,256]{1,0:T(8,128)}, u32[]{:S(2)}, u32[]{:S(2)}) collective-permute-start(f32[10,256]{1,0:T(8,128)} %stack.30), channel_id=1, source_target_pairs={{0,64},{32,96},{64,128},{96,160},{128,192},{160,224},{1,65},{33,97... | collective-permute-start | bytes 30728 | tf_op jit(solution)/shard_map/ppermute | solution.py:23
  78.1 1.2 stack.31
  79.4 1.3 collective-permute-start.11
  80.7 9.7 %collective-permute-start.10 = (f32[10,256]{1,0:T(8,128)}, f32[10,256]{1,0:T(8,128)}, u32[]{:S(2)}, u32[]{:S(2)}) collective-permute-start(f32[10,256]{1,0:T(8,128)} %stack.31), channel_id=1, source_target_pairs={{0,128},{32,160},{64,192},{96,224},{1,129},{33,161},{65,193},{97,2... | collective-permute-start | bytes 30728 | tf_op jit(solution)/shard_map/ppermute | solution.py:23
  90.4 1.6 slice_reduce_fusion.33
  93.8 1.6 slice_reduce_fusion.35
  120.8 2.4 %add_subtract_fusion.3 = (f32[8,32,1]{2,0,1:T(8,128)}, f32[8,32,1]{2,0,1:T(8,128)S(1)}, f32[8,32,1]{2,0,1:T(8,128)S(1)}, f32[8,32,1]{2,0,1:T(8,128)S(1)}, f32[8,...) fusion(f32[8,32,1]{2,0,1:T(8,128)S(1)} %copy.199, f32[8,32,1]{2,0,1:T(8,128)} %copy.198, ...), kind=kLoop, calls=%fused_computation.189 | loop fusion | flops 16640 | bytes 36864 | tf_op jit(solution)/shard_map/sub | solution.py:122
  134.8 2.2 %multiply_add_fusion.4 = (f32[8,32,1]{2,0,1:T(8,128)}, f32[8,32,1]{2,0,1:T(8,128)S(1)}, f32[8,32,1]{2,0,1:T(8,128)S(1)}, f32[8,32,1]{2,0,1:T(8,128)S(1)}, f32[8,...) fusion(f32[8,32,1]{2,0,1:T(8,128)} %get-tuple-element.509, f32[8,32,1]{2,0,1:T(8,128)S(1)} %copy.175, ...), kind=kLoop, calls=%fused_computation.185 | loop fusion | flops 16128 | bytes 33792 | tf_op jit(solution)/shard_map/add | solution.py:80
  141.4 15.3 %all-gather = f32[10,8192]{1,0:T(8,128)S(1)} all-gather(f32[10,1024]{1,0:T(8,128)S(1)} %stack.32), channel_id=2, replica_groups=mesh['gx'=8,'gy'=8,'gz'=4] {'gy'}, dimensions={1}, use_global_device_ids=true | all-gather | bytes 368640 | tf_op jit(solution)/shard_map/all_gather | solution.py:240
  163.2 15.4 %all-gather.1 = f32[10,16384]{1,0:T(8,128)S(1)} all-gather(f32[10,4096]{1,0:T(8,128)S(1)} %stack.36), channel_id=3, replica_groups=mesh['gx'=8,'gy'=8,'gz'=4] {'gz'}, dimensions={1}, use_global_device_ids=true | all-gather | bytes 819200 | tf_op jit(solution)/shard_map/all_gather | solution.py:245
  178.6 1.7 slice_reduce_fusion.1
  183.4 1.5 reshape.1806
  184.9 1.5 reshape.1807
  (573 shorter events, 95.5 us)
Async XLA Ops:
  1.2 8.5 %collective-permute-start.1 = (f32[2,8,32,1]{3,2,1,0:T(8,128)S(1)}, f32[2,8,32,1]{3,2,1,0:T(8,128)S(1)}, u32[]{:S(2)}, u32[]{:S(2)}) collective-permute-start(f32[2,8,32,1]{3,2,1,0:T(8,128)S(1)} %get-tuple-element.563), channel_id=1, source_target_pairs={{32,0},{64,32},{96,64},{128,96},{160,128},{192,160},{224,192},{33,... | collective-permute-start | bytes 6152 | tf_op jit(solution)/shard_map/ppermute | solution.py:15
  2.5 8.3 %collective-permute-start = (f32[2,8,32,1]{3,2,1,0:T(8,128)S(1)}, f32[2,8,32,1]{3,2,1,0:T(8,128)S(1)}, u32[]{:S(2)}, u32[]{:S(2)}) collective-permute-start(f32[2,8,32,1]{3,2,1,0:T(8,128)S(1)} %get-tuple-element.562), channel_id=1, source_target_pairs={{0,32},{32,64},{64,96},{96,128},{128,160},{160,192},{192,224},{1,3... | collective-permute-start | bytes 6152 | tf_op jit(solution)/shard_map/ppermute | solution.py:14
  7.6 13.5 %copy-start.46 = (f32[32]{0:T(128)}, f32[32]{0:T(128)S(1)}, u32[]{:S(2)}) copy-start(f32[32]{0:T(128)S(1)} %fusion.44) | copy-start | bytes 388
  7.6 23.4 %copy-start.59 = (pred[8]{0:T(512)(128)(4,1)}, pred[8]{0:T(512)(128)(4,1)S(1)}, u32[]{:S(2)}) copy-start(pred[8]{0:T(512)(128)(4,1)S(1)} %get-tuple-element.791) | copy-start | bytes 28
  8.8 22.2 %copy-start.61 = (pred[8]{0:T(512)(128)(4,1)}, pred[8]{0:T(512)(128)(4,1)S(1)}, u32[]{:S(2)}) copy-start(pred[8]{0:T(512)(128)(4,1)S(1)} %get-tuple-element.801) | copy-start | bytes 28
  8.8 22.2 %copy-start.64 = (pred[32]{0:T(512)(128)(4,1)}, pred[32]{0:T(512)(128)(4,1)S(1)}, u32[]{:S(2)}) copy-start(pred[32]{0:T(512)(128)(4,1)S(1)} %get-tuple-element.793) | copy-start | bytes 100
  12.1 8.7 %collective-permute-start.2 = (f32[2,8,1,130]{3,1,2,0:T(8,128)S(1)}, f32[2,8,1,130]{3,1,2,0:T(8,128)S(1)}, u32[]{:S(2)}, u32[]{:S(2)}) collective-permute-start(f32[2,8,1,130]{3,1,2,0:T(8,128)S(1)} %copy.222), channel_id=1, source_target_pairs={{0,4},{4,8},{8,12},{12,16},{16,20},{20,24},{24,28},{1,5},{5,9},{9,... | collective-permute-start | bytes 24968 | tf_op jit(solution)/shard_map/ppermute | solution.py:14
  18.9 12.2 %copy-start.66 = (pred[32]{0:T(512)(128)(4,1)}, pred[32]{0:T(512)(128)(4,1)S(1)}, u32[]{:S(2)}) copy-start(pred[32]{0:T(512)(128)(4,1)S(1)} %get-tuple-element.799) | copy-start | bytes 100
  18.9 5.0 %collective-permute-start.3 = (f32[2,8,1,130]{3,1,2,0:T(8,128)S(1)}, f32[2,8,1,130]{3,1,2,0:T(8,128)S(1)}, u32[]{:S(2)}, u32[]{:S(2)}) collective-permute-start(f32[2,8,1,130]{3,1,2,0:T(8,128)S(1)} %copy.223), channel_id=1, source_target_pairs={{4,0},{8,4},{12,8},{16,12},{20,16},{24,20},{28,24},{5,1},{9,5},{13... | collective-permute-start | bytes 24968 | tf_op jit(solution)/shard_map/ppermute | solution.py:15
  24.0 5.5 %collective-permute-start.5 = (f32[2,1,34,130]{3,1,2,0:T(1,128)S(1)}, f32[2,1,34,130]{3,1,2,0:T(1,128)S(1)}, u32[]{:S(2)}, u32[]{:S(2)}) collective-permute-start(f32[2,1,34,130]{3,1,2,0:T(1,128)S(1)} %get-tuple-element.452), channel_id=1, source_target_pairs={{1,0},{2,1},{3,2},{5,4},{6,5},{7,6},{9,8},{10,9},{11,10},{13,12},{... | collective-permute-start | bytes 106088 | tf_op jit(solution)/shard_map/ppermute | solution.py:15
  25.3 5.3 %collective-permute-start.4 = (f32[2,1,34,130]{3,1,2,0:T(1,128)S(1)}, f32[2,1,34,130]{3,1,2,0:T(1,128)S(1)}, u32[]{:S(2)}, u32[]{:S(2)}) collective-permute-start(f32[2,1,34,130]{3,1,2,0:T(1,128)S(1)} %get-tuple-element.451), channel_id=1, source_target_pairs={{0,1},{1,2},{2,3},{4,5},{5,6},{6,7},{8,9},{9,10},{10,11},{12,13},{... | collective-permute-start | bytes 106088 | tf_op jit(solution)/shard_map/ppermute | solution.py:14
  29.3 18.9 %copy-start.44 = (f32[8]{0:T(128)}, f32[8]{0:T(128)S(1)}, u32[]{:S(2)}) copy-start(f32[8]{0:T(128)S(1)} %fusion.47) | copy-start | bytes 100
  42.2 10.9 %collective-permute-start.7 = (f32[10,256]{1,0:T(8,128)S(1)}, f32[10,256]{1,0:T(8,128)S(1)}, u32[]{:S(2)}, u32[]{:S(2)}) collective-permute-start(f32[10,256]{1,0:T(8,128)S(1)} %stack.29), channel_id=1, source_target_pairs={{32,0},{64,32},{96,64},{128,96},{160,128},{192,160},{224,192},{33,... | collective-permute-start | bytes 30728 | tf_op jit(solution)/shard_map/ppermute | solution.py:23
  43.5 9.6 %collective-permute-start.6 = (f32[10,256]{1,0:T(8,128)S(1)}, f32[10,256]{1,0:T(8,128)S(1)}, u32[]{:S(2)}, u32[]{:S(2)}) collective-permute-start(f32[10,256]{1,0:T(8,128)S(1)} %stack.29), channel_id=1, source_target_pairs={{0,32},{32,64},{64,96},{96,128},{128,160},{160,192},{192,224},{1,3... | collective-permute-start | bytes 30728 | tf_op jit(solution)/shard_map/ppermute | solution.py:23
  53.1 12.3 %copy-start.36 = (f32[1,256]{1,0:T(1,128)}, f32[1,256]{1,0:T(1,128)S(1)}, u32[]{:S(2)}) copy-start(f32[1,256]{1,0:T(1,128)S(1)} %get-tuple-element.356) | copy-start | bytes 3076
  53.1 12.3 %copy-start.38 = (f32[1,256]{1,0:T(1,128)}, f32[1,256]{1,0:T(1,128)S(1)}, u32[]{:S(2)}) copy-start(f32[1,256]{1,0:T(1,128)S(1)} %get-tuple-element.364) | copy-start | bytes 3076
  53.2 12.3 %copy-start.28 = (f32[1,256]{1,0:T(1,128)}, f32[1,256]{1,0:T(1,128)S(1)}, u32[]{:S(2)}) copy-start(f32[1,256]{1,0:T(1,128)S(1)} %get-tuple-element.745) | copy-start | bytes 3076
  53.2 12.2 %copy-start.30 = (f32[1,256]{1,0:T(1,128)}, f32[1,256]{1,0:T(1,128)S(1)}, u32[]{:S(2)}) copy-start(f32[1,256]{1,0:T(1,128)S(1)} %get-tuple-element.746) | copy-start | bytes 3076
  53.2 12.2 %copy-start.32 = (f32[1,256]{1,0:T(1,128)}, f32[1,256]{1,0:T(1,128)S(1)}, u32[]{:S(2)}) copy-start(f32[1,256]{1,0:T(1,128)S(1)} %get-tuple-element.753) | copy-start | bytes 3076
  53.2 12.2 %copy-start.34 = (f32[1,256]{1,0:T(1,128)}, f32[1,256]{1,0:T(1,128)S(1)}, u32[]{:S(2)}) copy-start(f32[1,256]{1,0:T(1,128)S(1)} %get-tuple-element.754) | copy-start | bytes 3076
  54.4 21.0 %collective-permute-start.9 = (f32[10,256]{1,0:T(8,128)}, f32[10,256]{1,0:T(8,128)}, u32[]{:S(2)}, u32[]{:S(2)}) collective-permute-start(f32[10,256]{1,0:T(8,128)} %stack.30), channel_id=1, source_target_pairs={{64,0},{96,32},{128,64},{160,96},{192,128},{224,160},{65,1},{97,33... | collective-permute-start | bytes 30728 | tf_op jit(solution)/shard_map/ppermute | solution.py:23
  55.7 19.8 %collective-permute-start.8 = (f32[10,256]{1,0:T(8,128)}, f32[10,256]{1,0:T(8,128)}, u32[]{:S(2)}, u32[]{:S(2)}) collective-permute-start(f32[10,256]{1,0:T(8,128)} %stack.30), channel_id=1, source_target_pairs={{0,64},{32,96},{64,128},{96,160},{128,192},{160,224},{1,65},{33,97... | collective-permute-start | bytes 30728 | tf_op jit(solution)/shard_map/ppermute | solution.py:23
  79.4 48.4 %collective-permute-start.11 = (f32[10,256]{1,0:T(8,128)}, f32[10,256]{1,0:T(8,128)}, u32[]{:S(2)}, u32[]{:S(2)}) collective-permute-start(f32[10,256]{1,0:T(8,128)} %stack.31), channel_id=1, source_target_pairs={{128,0},{160,32},{192,64},{224,96},{129,1},{161,33},{193,65},{225,... | collective-permute-start | bytes 30728 | tf_op jit(solution)/shard_map/ppermute | solution.py:23
  80.7 48.5 %collective-permute-start.10 = (f32[10,256]{1,0:T(8,128)}, f32[10,256]{1,0:T(8,128)}, u32[]{:S(2)}, u32[]{:S(2)}) collective-permute-start(f32[10,256]{1,0:T(8,128)} %stack.31), channel_id=1, source_target_pairs={{0,128},{32,160},{64,192},{96,224},{1,129},{33,161},{65,193},{97,2... | collective-permute-start | bytes 30728 | tf_op jit(solution)/shard_map/ppermute | solution.py:23
  (64 other events, 168.5 us)
where the time goes:
time: 194 us; the launch traced here: 191 us
  local copies, waits for them, and re-layouts  77.4 us (40%)
  starting transfers between devices  44.8 us (23%)
  blocking collectives  30.8 us (16%)
  other arithmetic  30.6 us (16%)
  waiting for transfers between devices  5.4 us (3%)
  between operations  2.55 us (1%)
    ppermute x6, starting transfers between devices, shifted(): lax.ppermute(value, axis, [(source, source + steps) for source in range(l...  25.1 us
    all_gather x1, blocking collectives, finish_z(): lax.all_gather(system[:, None], 'gz', axis=1, tiled=True)  15.4 us
    all_gather x1, blocking collectives, finish_y(): lax.all_gather(system[:, None], 'gy', axis=1, tiled=True)  15.3 us
    ppermute x3, starting transfers between devices, extended(): before = lax.ppermute(last, axis, up)  15.2 us
    unnamed x157, local copies, waits for them, and re-layouts  8.05 us
    slice x6, local copies, waits for them, and re-layouts, split_system(): system[8]  7.31 us
    unnamed x45, other arithmetic  6.44 us
    squeeze x10, local copies, waits for them, and re-layouts, split_system(): system[8]  6.29 us
  transfers between devices with their start and end apart: 12, of which 4 were waited for; matrix products, arithmetic and copies ran while one was open for 29% of the time, Pallas kernels for 0%

commit v1 on v0

v1 whole, which is shorter than its diff:
```python
import functools

import jax
import jax.numpy as jnp
from jax import lax
from jax.experimental import pallas as pl
from jax.experimental.pallas import tpu as pltpu
from jax.sharding import PartitionSpec as P

MESH = pl.DeviceIdType.MESH
NZ, NY, NX = 8, 32, 128
GROUP = 4


def rcp(x):
    return 1.0 / x


def edge(a, b):
    return a * b * rcp(a + b)


def lane_roll(x, by):
    return pltpu.roll(x, by % NX, x.ndim - 1)


class Gather:
    def __init__(self, axis, count, buf, send, recv):
        self.axis, self.count, self.buf, self.send, self.recv = axis, count, buf, send, recv
        self.me = lax.axis_index(axis)

    def copy(self, slot, peer, step):
        return pltpu.make_async_remote_copy(
            src_ref=self.buf.at[slot],
            dst_ref=self.buf.at[slot],
            send_sem=self.send.at[step - 1],
            recv_sem=self.recv.at[slot],
            device_id={self.axis: peer},
            device_id_type=MESH,
        )

    def start(self):
        for step in range(1, self.count):
            self.copy(self.me, lax.rem(self.me + step, self.count), step).start()

    def wait_recv(self):
        for step in range(1, self.count):
            peer = lax.rem(self.me + step, self.count)
            self.copy(peer, peer, step).wait_recv()

    def wait_send(self):
        for step in range(1, self.count):
            self.copy(self.me, lax.rem(self.me + step, self.count), step).wait_send()


class Halo:
    def __init__(self, axis, count, low, high, buf, send, recv):
        self.axis, self.count, self.buf, self.send, self.recv = axis, count, buf, send, recv
        self.me = lax.axis_index(axis)
        self.ends = (high, low)

    def copy(self, side):
        step = (1, self.count - 1)[side]
        return pltpu.make_async_remote_copy(
            src_ref=self.ends[side],
            dst_ref=self.buf.at[side],
            send_sem=self.send.at[side],
            recv_sem=self.recv.at[side],
            device_id={self.axis: lax.rem(self.me + step, self.count)},
            device_id_type=MESH,
        )

    def start(self):
        for side in range(2):
            self.copy(side).start()

    def wait_recv(self):
        for side in range(2):
            self.copy(side).wait_recv()

    def wait_send(self):
        for side in range(2):
            self.copy(side).wait_send()


def chain_matrix(edges, store_rho, store_inv, store_p, store_q):
    last = len(edges)
    looking = edges[last - 1]
    rhos = [None] * last
    for i in range(last - 2, -1, -1):
        inv = rcp(edges[i] + (1.0 + looking))
        rhos[i] = edges[i] * inv
        store_rho(i, rhos[i])
        store_inv(i, inv)
        looking = rhos[i] * (1.0 + looking)
    looking = edges[0]
    lambdas = [None] * (last + 1)
    for i in range(2, last + 1):
        lambdas[i] = edges[i - 1] * rcp(edges[i - 1] + (1.0 + looking))
        looking = lambdas[i] * (1.0 + looking)
    one = jnp.ones_like(edges[0])
    zero = jnp.zeros_like(one)
    store_p(0, one)
    store_p(last, zero)
    store_q(0, zero)
    store_q(last, one)
    resp, ground_first = one, one
    for i in range(last - 1):
        resp = rhos[i] * resp
        store_p(i + 1, resp)
        ground_first = ground_first + resp
    resp, ground_last = one, one
    for i in range(last, 1, -1):
        resp = lambdas[i] * resp
        store_q(i - 1, resp)
        ground_last = ground_last + resp
    return ground_first, ground_last, edges[0] * resp


def chain_base(length, side, rho, inv, store):
    sums = [None] * length
    total = side(length - 2)
    sums[length - 2] = total
    for i in range(length - 3, 0, -1):
        total = side(i) + rho(i) * total
        sums[i] = total
    value = inv(0) * sums[1]
    store(1, value)
    for i in range(1, length - 2):
        value = rho(i) * value + inv(i) * sums[i + 1]
        store(i + 1, value)


def device_chain(count, me, ground_first, ground_last, inner, face):
    up_inner, up_face, gf = [None] * count, [None] * (count + 1), [None] * count
    gf[0] = ground_first[0]
    for q in range(count):
        up_inner[q] = inner[q] * rcp(inner[q] + gf[q])
        if q < count - 1:
            behind = ground_last[q] + up_inner[q] * gf[q]
            up_face[q + 1] = face[q + 1] * rcp(face[q + 1] + behind)
            gf[q + 1] = ground_first[q + 1] + up_face[q + 1] * behind
    down_inner, down_face, gl = [None] * count, [None] * (count + 1), [None] * count
    gl[count - 1] = ground_last[count - 1]
    for q in range(count - 1, -1, -1):
        down_inner[q] = inner[q] * rcp(inner[q] + gl[q])
        if q > 0:
            behind = ground_first[q] + down_inner[q] * gl[q]
            down_face[q] = face[q] * rcp(face[q] + behind)
            gl[q - 1] = ground_last[q - 1] + down_face[q] * behind
    zero = jnp.zeros_like(gf[0])

    def own(values):
        out = zero
        for q in range(count):
            if values[q] is not None:
                out = jnp.where(me == q, values[q], out)
        return out

    own_f, own_l, own_i = own(gf), own(gl), own(inner)
    scale = rcp(own_f * (own_l + own_i) + own_i * own_l)
    aa, bb, cc = (own_l + own_i) * scale, (own_f + own_i) * scale, own_i * scale
    from_low_f, from_low_l = [zero] * count, [zero] * count
    via_low = [zero] * count
    carry = zero
    for q in range(count - 2, -1, -1):
        via_low[q] = jnp.where(me == q + 1, 1.0, carry)
        from_low_l[q] = via_low[q] * up_face[q + 1]
        from_low_f[q] = from_low_l[q] * up_inner[q]
        carry = from_low_f[q]
    from_high_f, from_high_l = [zero] * count, [zero] * count
    via_high = [zero] * count
    carry = zero
    for q in range(1, count):
        via_high[q] = jnp.where(me == q - 1, 1.0, carry)
        from_high_f[q] = via_high[q] * down_face[q]
        from_high_l[q] = from_high_f[q] * down_inner[q]
        carry = from_high_l[q]
    return dict(
        aa=aa, bb=bb, cc=cc,
        low_f=from_low_f, low_l=from_low_l, high_f=from_high_f, high_l=from_high_l,
        via_low=via_low, via_high=via_high,
        up_inner=own(up_inner), up_face=own(up_face[1:]), down_inner=own(down_inner), down_face=own(down_face[:count]),
    )


def kernel(counts, t_hbm, c_hbm, out_ref, s):
    nx, ny, nz = counts
    mx, my, mz = lax.axis_index("gx"), lax.axis_index("gy"), lax.axis_index("gz")
    lane = lax.broadcasted_iota(jnp.int32, (NZ, NX), 1)

    barrier = pltpu.get_barrier_semaphore()
    for axis, me, count in (("gz", mz, nz), ("gy", my, ny), ("gx", mx, nx)):
        for step in range(1, count):
            pl.semaphore_signal(
                barrier, inc=1, device_id={axis: lax.rem(me + step, count)}, device_id_type=MESH
            )
    load_t = pltpu.make_async_copy(t_hbm, s["tc"].at[0], s["load"].at[0])
    load_c = pltpu.make_async_copy(c_hbm, s["tc"].at[1], s["load"].at[1])
    load_t.start()
    load_c.start()

    tc = s["tc"]
    halo_z = Halo("gz", nz, tc.at[:, pl.ds(0, NY)], tc.at[:, pl.ds((NZ - 1) * NY, NY)], s["hz"], s["hz_s"], s["hz_r"])
    halo_y = Halo("gy", ny, s["ey"].at[0], s["ey"].at[1], s["hy"], s["hy_s"], s["hy_r"])
    info_x = Gather("gx", nx, s["ix"], s["ix_s"], s["ix_r"])
    info_y = Gather("gy", ny, s["iy"], s["iy_s"], s["iy_r"])
    info_z = Gather("gz", nz, s["iz"], s["iz_s"], s["iz_r"])
    side_x = Gather("gx", nx, s["bx"], s["bx_s"], s["bx_r"])
    side_y = Gather("gy", ny, s["by"], s["by_s"], s["by_r"])
    side_z = Gather("gz", nz, s["bz"], s["bz_s"], s["bz_r"])

    load_t.wait()
    load_c.wait()
    for side, y in ((0, 0), (1, NY - 1)):
        for k in range(2):
            s["ey"][side, k] = tc[k, pl.ds(y, NZ, stride=NY), :]
    pl.semaphore_wait(barrier, nx + ny + nz - 3)
    halo_y.start()
    halo_z.start()

    info_a, info_b = jnp.zeros((NZ, NX), jnp.float32), jnp.zeros((NZ, NX), jnp.float32)
    for y0 in range(0, NY, GROUP):
        rows = pl.ds(y0, GROUP)
        t = jnp.stack([tc[0, pl.ds(y, NZ, stride=NY), :] for y in range(y0, y0 + GROUP)])
        c = jnp.stack([tc[1, pl.ds(y, NZ, stride=NY), :] for y in range(y0, y0 + GROUP)])
        s["ty"][rows] = t
        s["cy"][rows] = c
        spot = lax.broadcasted_iota(jnp.int32, t.shape, 2)
        e_high = edge(c, lane_roll(c, -1))
        e_low = lane_roll(e_high, 1)
        flux = jnp.where(spot == NX - 1, 0.0, 2.0 * e_high * (lane_roll(t, -1) - t))
        s["fx"][rows] = t + 0.5 * (flux - lane_roll(flux, 1))
        inv = rcp(1.0 + e_low + e_high)
        is_first, is_last = spot == 0, spot == NX - 1
        gnd = jnp.where(is_first | is_last, 0.0, inv)
        low = jnp.where(is_first, 1.0, jnp.where(is_last, 0.0, e_low * inv))
        high = jnp.where(is_last, 1.0, jnp.where(is_first, 0.0, e_high * inv))
        s["x_inv"][rows] = gnd
        for level in range(7):
            k = 1 << level
            no_low, no_high = spot < k, spot >= NX - k
            gnd_m = jnp.where(no_low, 0.0, lane_roll(gnd, k))
            low_m = jnp.where(no_low, 1.0, lane_roll(low, k))
            gnd_p = jnp.where(no_high, 0.0, lane_roll(gnd, -k))
            high_p = jnp.where(no_high, 1.0, lane_roll(high, -k))
            keep = rcp(gnd + low * (gnd_m + low_m) + high * (gnd_p + high_p))
            take_low, take_high = low * keep, high * keep
            s["x_keep"][level, rows] = keep
            s["x_low"][level, rows] = jnp.where(no_low, 0.0, take_low)
            s["x_high"][level, rows] = jnp.where(no_high, 0.0, take_high)
            gnd = gnd * keep + take_low * gnd_m + take_high * gnd_p
            low = take_low * low_m
            high = take_high * high_p
        s["x_p"][rows] = low
        s["x_q"][rows] = high
        ground = jnp.where(spot == 1, e_low, e_high) * gnd
        joint = e_low * high
        for j in range(GROUP):
            y = y0 + j
            for at, value, source in ((0, t, 0), (32, t, NX - 1), (64, c, 0), (96, c, NX - 1)):
                info_a = jnp.where(lane == at + y, lane_roll(value[j], at + y - source), info_a)
            for at, value, source in ((0, ground, 1), (32, ground, NX - 2), (64, joint, 1)):
                info_b = jnp.where(lane == at + y, lane_roll(value[j], at + y - source), info_b)
    s["ix"][mx, 0] = info_a
    s["ix"][mx, 1] = info_b + jnp.where(lane < 64, 1.0, 0.0)
    info_x.start()

    tz = [tc[0, pl.ds(z * NY, NY), :] for z in range(NZ)]
    cz = [tc[1, pl.ds(z * NY, NY), :] for z in range(NZ)]
    edges_z = [edge(cz[z], cz[z + 1]) for z in range(NZ - 1)]
    flux_z = [2.0 * edges_z[z] * (tz[z + 1] - tz[z]) for z in range(NZ - 1)]
    for z in range(NZ):
        lap = (flux_z[z] if z < NZ - 1 else 0.0) - (flux_z[z - 1] if z > 0 else 0.0)
        s["lz"][z] = lap
        if z < NZ - 1:
            s["ez"][z] = edges_z[z]
        if 0 < z < NZ - 1:
            for tile in range(NY // 8):
                s["lzy"][pl.ds(tile * 64 + z, 8, stride=8), :] = lap[tile * 8:tile * 8 + 8]
    below = None
    for y in range(NY):
        lap = 0.0
        if y < NY - 1:
            e = edge(s["cy"][y], s["cy"][y + 1])
            s["eyy"][y] = e
            above = 2.0 * e * (s["ty"][y + 1] - s["ty"][y])
            lap = above
        if y > 0:
            lap = lap - below
        below = above
        s["ly"][y] = lap

    halo_y.wait_recv()
    halo_z.wait_recv()
    wall_y, wall_z = [], []
    for side, me, count in ((0, my, ny), (1, my, ny)):
        at_wall = me == (0, count - 1)[side]
        y = (0, NY - 1)[side]
        t_end, c_end = s["ty"][y], s["cy"][y]
        face = jnp.where(at_wall, c_end, edge(s["hy"][side, 1], c_end))
        beyond = jnp.where(at_wall, 0.0, s["hy"][side, 0])
        s["ly"][y] = s["ly"][y] + 2.0 * face * (beyond - t_end)
        wall_y.append((at_wall, face))
    for side in range(2):
        at_wall = mz == (0, nz - 1)[side]
        z = (0, NZ - 1)[side]
        t_end, c_end = tc[0, pl.ds(z * NY, NY), :], tc[1, pl.ds(z * NY, NY), :]
        face = jnp.where(at_wall, c_end, edge(s["hz"][side, 1], c_end))
        beyond = jnp.where(at_wall, 0.0, s["hz"][side, 0])
        lap = s["lz"][z] + 2.0 * face * (beyond - t_end)
        s["lz"][z] = lap
        for tile in range(NY // 8):
            s["lzy"][pl.ds(tile * 64 + z, 8, stride=8), :] = lap[tile * 8:tile * 8 + 8]
        wall_z.append((at_wall, face))

    packed = jnp.zeros((NZ, NX), jnp.float32)
    for y in range(NY):
        f = s["fx"][y] + s["ly"][y] + s["lzy"][pl.ds(y * 8, 8), :]
        s["fx"][y] = f
        first = jnp.sum(s["x_p"][y] * f, axis=1, keepdims=True)
        final = jnp.sum(s["x_q"][y] * f, axis=1, keepdims=True)
        packed = jnp.where(lane == y, first, jnp.where(lane == 32 + y, final, packed))
    s["bx"][mx] = packed
    side_x.start()

    edges_y = [s["eyy"][y] for y in range(NY - 1)]

    def put(name):
        def store(i, value):
            s[name][i] = value
        return store

    g_first, g_last, joint = chain_matrix(edges_y, put("y_rho"), put("y_inv"), put("y_p"), put("y_q"))
    (wall_low, face_low), (wall_high, face_high) = wall_y
    s["iy"][my, 0] = g_first + jnp.where(wall_low, face_low, 0.0)
    s["iy"][my, 1] = g_last + jnp.where(wall_high, face_high, 0.0)
    s["iy"][my, 2] = joint
    s["iy"][my, 3] = face_low
    info_y.start()
    g_first, g_last, joint = chain_matrix(
        [s["ez"][z] for z in range(NZ - 1)], put("z_rho"), put("z_inv"), put("z_p"), put("z_q")
    )
    (wall_low, face_low), (wall_high, face_high) = wall_z
    s["iz"][mz, 0] = g_first + jnp.where(wall_low, face_low, 0.0)
    s["iz"][mz, 1] = g_last + jnp.where(wall_high, face_high, 0.0)
    s["iz"][mz, 2] = joint
    s["iz"][mz, 3] = face_low
    info_z.start()

    for y0 in range(0, NY, GROUP):
        rows = pl.ds(y0, GROUP)
        f = s["fx"][rows] * s["x_inv"][rows]
        for level in range(7):
            k = 1 << level
            f = (
                s["x_keep"][level, rows] * f
                + s["x_low"][level, rows] * lane_roll(f, k)
                + s["x_high"][level, rows] * lane_roll(f, -k)
            )
        s["fx"][rows] = f

    info_x.wait_recv()
    parts = []
    for q in range(nx):
        a, b = s["ix"][q, 0], s["ix"][q, 1]
        parts.append([a, lane_roll(a, -32), lane_roll(a, -64), lane_roll(a, -96), b, lane_roll(b, -32), lane_roll(b, -64)])
    faces = [None] * nx
    add_f, add_l = [None] * nx, [None] * nx
    gf, gl = [p[4] for p in parts], [p[5] for p in parts]
    add_f[0] = -parts[0][2] * parts[0][0]
    gf[0] = gf[0] + parts[0][2]
    add_l[nx - 1] = -parts[nx - 1][3] * parts[nx - 1][1]
    gl[nx - 1] = gl[nx - 1] + parts[nx - 1][3]
    for q in range(1, nx):
        faces[q] = edge(parts[q - 1][3], parts[q][2])
        flow = faces[q] * (parts[q][0] - parts[q - 1][1])
        add_f[q] = -flow
        add_l[q - 1] = flow
    ch = device_chain(nx, mx, gf, gl, [p[6] for p in parts], faces)
    const_f, const_l = 0.0, 0.0
    for q in range(nx):
        here = jnp.where(mx == q, 1.0, 0.0)
        lf, ll = ch["low_f"][q] + here, ch["low_l"][q]
        hf, hl = ch["high_f"][q], ch["high_l"][q] + here
        ff, fl = ch["aa"] * lf + ch["cc"] * hf, ch["aa"] * ll + ch["cc"] * hl
        lf, ll = ch["cc"] * lf + ch["bb"] * hf, ch["cc"] * ll + ch["bb"] * hl
        const_f = const_f + ff * add_f[q] + fl * add_l[q]
        const_l = const_l + lf * add_f[q] + ll * add_l[q]
        s["wx"][q, 0] = jnp.where(lane < 32, ff, lane_roll(fl, 32))
        s["wx"][q, 1] = jnp.where(lane < 32, lf, lane_roll(ll, 32))
    side_x.wait_recv()
    first, final = 0.0, 0.0
    for q in range(nx):
        b = jnp.where(lane < 64, s["bx"][q], 0.0)
        first = first + jnp.where(lane < 64, s["wx"][q, 0], 0.0) * b
        final = final + jnp.where(lane < 64, s["wx"][q, 1], 0.0) * b
    first = first + lane_roll(first, -32) + const_f
    final = final + lane_roll(final, -32) + const_l

    sum_first, sum_last = 0.0, 0.0
    for y in range(NY):
        u = (
            s["fx"][y]
            + s["x_p"][y] * jnp.broadcast_to(first[:, y:y + 1], (NZ, NX))
            + s["x_q"][y] * jnp.broadcast_to(final[:, y:y + 1], (NZ, NX))
        )
        f = u - 0.5 * s["ly"][y]
        s["fy"][y] = f
        sum_first = sum_first + s["y_p"][y] * f
        sum_last = sum_last + s["y_q"][y] * f

    def reduced_weights(info, buf, count, me):
        info.wait_recv()
        ch = device_chain(
            count, me, *[[buf[q, k] for q in range(count)] for k in range(4)]
        )
        to_f = [ch["aa"] * ch["via_low"][q] + ch["cc"] * ch["via_high"][q] for q in range(count)]
        to_l = [ch["cc"] * ch["via_low"][q] + ch["bb"] * ch["via_high"][q] for q in range(count)]
        return ch, to_f, to_l

    ch, to_f, to_l = reduced_weights(info_y, s["iy"], ny, my)
    s["by_out"][0] = ch["up_face"] * (sum_last + ch["up_inner"] * sum_first)
    s["by_out"][1] = ch["down_face"] * (sum_first + ch["down_inner"] * sum_last)

    def send_ends(axis, me, count, out, gather):
        for step in range(1, count):
            peer = lax.rem(me + step, count)
            pltpu.make_async_remote_copy(
                src_ref=out.at[jnp.where(peer > me, 0, 1)],
                dst_ref=gather.buf.at[me],
                send_sem=gather.send.at[step - 1],
                recv_sem=gather.recv.at[me],
                device_id={axis: peer},
                device_id_type=MESH,
            ).start()

    send_ends("gy", my, ny, s["by_out"], side_y)
    s["by"][my] = jnp.zeros((NZ, NX), jnp.float32)

    def load(name):
        return lambda i: s[name][i]

    chain_base(NY, load("fy"), load("y_rho"), load("y_inv"), put("yb"))
    s["yb"][0] = jnp.zeros((NZ, NX), jnp.float32)
    s["yb"][NY - 1] = jnp.zeros((NZ, NX), jnp.float32)
    first = ch["aa"] * sum_first + ch["cc"] * sum_last
    final = ch["cc"] * sum_first + ch["bb"] * sum_last
    side_y.wait_recv()
    for q in range(ny):
        b = s["by"][q]
        first = first + to_f[q] * b
        final = final + to_l[q] * b
    for y in range(NY):
        s["u2"][pl.ds(y * 8, 8), :] = s["yb"][y] + s["y_p"][y] * first + s["y_q"][y] * final

    ch, to_f, to_l = reduced_weights(info_z, s["iz"], nz, mz)
    sum_first, sum_last = 0.0, 0.0
    for z in range(NZ):
        u = jnp.concatenate([s["u2"][pl.ds(tile * 64 + z, 8, stride=8), :] for tile in range(NY // 8)], axis=0)
        f = u - 0.5 * s["lz"][z]
        s["fz"][z] = f
        sum_first = sum_first + s["z_p"][z] * f
        sum_last = sum_last + s["z_q"][z] * f
    s["bz_out"][0] = ch["up_face"] * (sum_last + ch["up_inner"] * sum_first)
    s["bz_out"][1] = ch["down_face"] * (sum_first + ch["down_inner"] * sum_last)
    send_ends("gz", mz, nz, s["bz_out"], side_z)
    s["bz"][mz] = jnp.zeros((NY, NX), jnp.float32)
    chain_base(NZ, load("fz"), load("z_rho"), load("z_inv"), put("zb"))
    s["zb"][0] = jnp.zeros((NY, NX), jnp.float32)
    s["zb"][NZ - 1] = jnp.zeros((NY, NX), jnp.float32)
    first = ch["aa"] * sum_first + ch["cc"] * sum_last
    final = ch["cc"] * sum_first + ch["bb"] * sum_last
    side_z.wait_recv()
    for q in range(nz):
        b = s["bz"][q]
        first = first + to_f[q] * b
        final = final + to_l[q] * b
    for z in range(NZ):
        out_ref[pl.ds(z * NY, NY), :] = s["zb"][z] + s["z_p"][z] * first + s["z_q"][z] * final

    for group in (halo_y, halo_z, info_x, info_y, info_z, side_x, side_y):
        group.wait_send()
    for step in range(1, nz):
        pltpu.make_async_remote_copy(
            src_ref=s["bz_out"].at[0], dst_ref=s["bz"].at[0], send_sem=side_z.send.at[step - 1],
            recv_sem=side_z.recv.at[0], device_id={"gz": lax.rem(mz + step, nz)}, device_id_type=MESH,
        ).wait_send()


def scratch(counts):
    nx, ny, nz = counts
    f32 = jnp.float32
    ycells, zcells = (NY, NZ, NX), (NZ, NY, NX)
    vmem = dict(
        tc=(2, NZ * NY, NX), ty=ycells, cy=ycells, fx=ycells, fy=ycells, ly=ycells, lz=zcells, fz=zcells,
        lzy=(NZ * NY, NX), u2=(NZ * NY, NX), eyy=ycells, ez=zcells,
        x_inv=ycells, x_p=ycells, x_q=ycells, x_keep=(7,) + ycells, x_low=(7,) + ycells, x_high=(7,) + ycells,
        y_rho=ycells, y_inv=ycells, y_p=ycells, y_q=ycells, yb=ycells,
        z_rho=zcells, z_inv=zcells, z_p=zcells, z_q=zcells, zb=zcells,
        ey=(2, 2, NZ, NX), hy=(2, 2, NZ, NX), hz=(2, 2, NY, NX),
        ix=(nx, 2, NZ, NX), bx=(nx, NZ, NX), wx=(nx, 2, NZ, NX),
        iy=(ny, 4, NZ, NX), by=(ny, NZ, NX), by_out=(2, NZ, NX),
        iz=(nz, 4, NY, NX), bz=(nz, NY, NX), bz_out=(2, NY, NX),
    )
    out = {name: pltpu.VMEM(shape, f32) for name, shape in vmem.items()}
    out["load"] = pltpu.SemaphoreType.DMA((2,))
    for name, count in (("hz", 2), ("hy", 2), ("ix", nx), ("iy", ny), ("iz", nz), ("bx", nx), ("by", ny), ("bz", nz)):
        out[name + "_s"] = pltpu.SemaphoreType.DMA((count,))
        out[name + "_r"] = pltpu.SemaphoreType.DMA((count,))
    return out


def solution(mesh):
    counts = (mesh.shape["gx"], mesh.shape["gy"], mesh.shape["gz"])
    shapes = scratch(counts)
    names = list(shapes)

    def body(t_hbm, c_hbm, out_ref, *refs):
        kernel(counts, t_hbm, c_hbm, out_ref, dict(zip(names, refs)))

    def on_device(thermal_state, diffusion_ratio):
        rows = NZ * NY
        out = pl.pallas_call(
            body,
            out_shape=jax.ShapeDtypeStruct((rows, NX), jnp.float32),
            in_specs=[pl.BlockSpec(memory_space=pl.ANY)] * 2,
            out_specs=pl.BlockSpec(memory_space=pltpu.VMEM),
            scratch_shapes=[shapes[name] for name in names],
            compiler_params=pltpu.CompilerParams(
                collective_id=0, has_side_effects=True, vmem_limit_bytes=24 * 1024 * 1024
            ),
        )(thermal_state.reshape(rows, NX), diffusion_ratio.reshape(rows, NX))
        return out.reshape(NZ, NY, NX)

    spec = P("gz", "gy", "gx")
    return jax.shard_map(on_device, mesh=mesh, in_specs=(spec, spec), out_specs=spec, check_vma=False)
```

time: 194 us -> 29.2 us (0.15); the launches traced: 191 us -> 29.1 us
  local copies, waits for them, and re-layouts: 77.4 us -> 2.47 us
  starting transfers between devices: 44.8 us -> 0 us
  blocking collectives: 30.8 us -> 0 us
  other arithmetic: 30.6 us -> 0 us
  Pallas kernels: 0 us -> 26.6 us
  waiting for transfers between devices: 5.4 us -> 0 us
  between operations: 2.55 us -> 0.01 us
    ppermute x12 -> x0, starting transfers between devices: 44.8 us -> none  [the longest x6 25.1 us: shifted(): lax.ppermute(value, axis, [(source, source + steps) for source in range(l...]
    squeeze x85 -> x0, local copies, waits for them, and re-layouts: 37.2 us -> none  [the longest x10 6.29 us: split_system(): system[8]]
    all_gather x2 -> x0, blocking collectives: 30.8 us -> none  [the longest x1 15.4 us: finish_z(): lax.all_gather(system[:, None], 'gz', axis=1, tiled=True)]
    pallas_call x0 -> x1, Pallas kernels: none -> 26.6 us  [on_device(): pl.pallas_call(body, out_shape=jax.ShapeDtypeStruct((rows, NX), jnp.float...]
    slice x126 -> x0, local copies, waits for them, and re-layouts: 17 us -> none  [the longest x6 7.31 us: split_system(): system[8]]
    sub x37 -> x0, other arithmetic: 8.26 us -> none  [the longest x15 2.73 us: local_solve(): side - factor_low * earlier(side, stride, axis_dim, 0.0)]
    another operation x30 -> x0, local copies, waits for them, and re-layouts: 7.17 us -> none  [the longest x2 2.46 us: block_step(): jnp.stack([-entry for entry in new_low] + [-entry for entry in new_high]...]
    unnamed x45 -> x0, other arithmetic: 6.44 us -> none
  transfers between devices with their start and end apart: 12 -> 0, of which waited for: 4 -> 0; matrix products, arithmetic and copies ran while one was open for 29% -> 0% of each run, Pallas kernels for 0% -> 0%
where the time goes in v1:
time: 29.2 us; the launch traced here: 29.1 us
  Pallas kernels  26.6 us (91%)
  local copies, waits for them, and re-layouts  2.47 us (8%)
    pallas_call x1, Pallas kernels, on_device(): pl.pallas_call(body, out_shape=jax.ShapeDtypeStruct((rows, NX), jnp.float...  26.6 us
    unnamed x5, local copies, waits for them, and re-layouts  2.47 us

profile of v1, /device:TPU:1, one launch (start us, length us, event | category | flops | bytes accessed | tf_op | source)
XLA Modules:
  0.0 29.1 jit_solution(16127078561634399408)
XLA Ops:
  0.0 0.0 copy-start
  0.0 0.9 %copy-done = f32[8,32,128]{2,1,0:T(8,128)S(1)} copy-done((f32[8,32,128]{2,1,0:T(8,128)S(1)}, f32[8,32,128]{2,1,0:T(8,128)}, u32[]{:S(2)}) %copy-start) | copy-done | bytes 131096
  0.9 0.0 copy-start.1
  0.9 0.9 %copy-done.1 = f32[8,32,128]{2,1,0:T(8,128)S(1)} copy-done((f32[8,32,128]{2,1,0:T(8,128)S(1)}, f32[8,32,128]{2,1,0:T(8,128)}, u32[]{:S(2)}) %copy-start.1) | copy-done | bytes 131096
  1.8 26.6 %shard_map.28 = f32[256,128]{1,0:T(8,128)S(1)} custom-call(f32[256,128]{1,0:T(8,128)S(1)} %bitcast.4, f32[256,128]{1,0:T(8,128)S(1)} %bitcast.5), custom_call_target="tpu_custom_call" | custom-call | tf_op jit(solution)/shard_map/pallas_call | solution.py:524
  28.4 0.7 %copy.4 = f32[8,32,128]{2,1,0:T(8,128)} copy(f32[8,32,128]{2,1,0:T(8,128)S(1)} %bitcast.3) | data formatting | bytes 262144
Async XLA Ops:
  0.0 0.9 %copy-start = (f32[8,32,128]{2,1,0:T(8,128)S(1)}, f32[8,32,128]{2,1,0:T(8,128)}, u32[]{:S(2)}) copy-start(f32[8,32,128]{2,1,0:T(8,128)} %param.2) | copy-start | bytes 393220
  0.9 0.9 %copy-start.1 = (f32[8,32,128]{2,1,0:T(8,128)S(1)}, f32[8,32,128]{2,1,0:T(8,128)}, u32[]{:S(2)}) copy-start(f32[8,32,128]{2,1,0:T(8,128)} %param.3) | copy-start | bytes 393220

commit v2 on v1

v2 whole, which is shorter than its diff:
```python
import functools

import jax
import jax.numpy as jnp
from jax import lax
from jax.experimental import pallas as pl
from jax.experimental.pallas import tpu as pltpu
from jax.sharding import PartitionSpec as P

MESH = pl.DeviceIdType.MESH
NZ, NY, NX = 8, 32, 128
SEG = 16


def rcp(x):
    return 1.0 / x


def edge(a, b):
    return a * b * rcp(a + b)


class Gather:
    def __init__(self, axis, count, buf, send, recv):
        self.axis, self.count, self.buf, self.send, self.recv = axis, count, buf, send, recv
        self.me = lax.axis_index(axis)
        self.steps = sorted(range(1, count), key=lambda step: -min(step, count - step))

    def copy(self, slot, peer, step):
        return pltpu.make_async_remote_copy(
            src_ref=self.buf.at[slot],
            dst_ref=self.buf.at[slot],
            send_sem=self.send.at[step - 1],
            recv_sem=self.recv.at[slot],
            device_id={self.axis: peer},
            device_id_type=MESH,
        )

    def start(self):
        for step in self.steps:
            self.copy(self.me, lax.rem(self.me + step, self.count), step).start()

    def wait_recv(self):
        for step in self.steps:
            peer = lax.rem(self.me + step, self.count)
            self.copy(peer, peer, step).wait_recv()

    def wait_send(self):
        for step in self.steps:
            self.copy(self.me, lax.rem(self.me + step, self.count), step).wait_send()


class Halo:
    def __init__(self, axis, count, low, high, buf, send, recv):
        self.axis, self.count, self.buf, self.send, self.recv = axis, count, buf, send, recv
        self.me = lax.axis_index(axis)
        self.ends = (high, low)

    def copy(self, side):
        step = (1, self.count - 1)[side]
        return pltpu.make_async_remote_copy(
            src_ref=self.ends[side],
            dst_ref=self.buf.at[side],
            send_sem=self.send.at[side],
            recv_sem=self.recv.at[side],
            device_id={self.axis: lax.rem(self.me + step, self.count)},
            device_id_type=MESH,
        )

    def start(self):
        for side in range(2):
            self.copy(side).start()

    def wait_recv(self):
        for side in range(2):
            self.copy(side).wait_recv()

    def wait_send(self):
        for side in range(2):
            self.copy(side).wait_send()


def near(count, reach):
    return sorted({s % count for r in range(1, reach + 1) for s in (r, -r)} - {0})


class Relay:
    def __init__(self, axis, count, reach, sem):
        self.axis, self.count, self.sem = axis, count, sem
        self.me = lax.axis_index(axis)
        self.rounds = []
        while reach < count // 2:
            self.rounds.append(reach)
            reach *= 2

    def fire(self, at):
        if at < len(self.rounds):
            for step in (self.rounds[at], self.count - self.rounds[at]):
                pl.semaphore_signal(
                    self.sem.at[at], inc=1, device_id={self.axis: lax.rem(self.me + step, self.count)},
                    device_id_type=MESH,
                )

    def wait(self, at):
        if at < len(self.rounds):
            pl.semaphore_wait(self.sem.at[at], 2)


def tree(values):
    values = list(values)
    while len(values) > 1:
        values = [sum(values[i:i + 2]) for i in range(0, len(values), 2)]
    return values[0]


def chain_matrix(edges, grounds, store_rho, store_inv, store_p, store_q):
    last = len(edges)
    rhos, lambdas = [None] * last, [None] * (last + 1)
    from_high, from_low = edges[last - 1], edges[0]
    for k in range(last - 1):
        i = last - 2 - k
        inv = rcp(edges[i] + (grounds[i + 1] + from_high))
        rhos[i] = edges[i] * inv
        store_rho(i, rhos[i])
        store_inv(i, inv)
        from_high = rhos[i] * (grounds[i + 1] + from_high)
        i = 2 + k
        lambdas[i] = edges[i - 1] * rcp(edges[i - 1] + (grounds[i - 1] + from_low))
        from_low = lambdas[i] * (grounds[i - 1] + from_low)
    one = jnp.ones_like(edges[0])
    zero = jnp.zeros_like(one)
    store_p(0, one)
    store_p(last, zero)
    store_q(0, zero)
    store_q(last, one)
    resp_p, ground_first = one, grounds[0]
    resp_q, ground_last = one, grounds[last]
    for k in range(last - 1):
        resp_p = rhos[k] * resp_p
        store_p(k + 1, resp_p)
        ground_first = ground_first + resp_p * grounds[k + 1]
        i = last - k
        resp_q = lambdas[i] * resp_q
        store_q(i - 1, resp_q)
        ground_last = ground_last + resp_q * grounds[i - 1]
    return ground_first, ground_last, edges[0] * resp_q


def chain_base(length, side, rho, inv, store):
    sums = [None] * length
    total = side(length - 2)
    sums[length - 2] = total
    for i in range(length - 3, 0, -1):
        total = side(i) + rho(i) * total
        sums[i] = total
    value = inv(0) * sums[1]
    store(1, value)
    for i in range(1, length - 2):
        value = rho(i) * value + inv(i) * sums[i + 1]
        store(i + 1, value)


def device_chain(count, me, ground_first, ground_last, inner, face):
    up_inner, up_face, gf = [None] * count, [None] * (count + 1), [None] * count
    gf[0] = ground_first[0]
    for q in range(count):
        up_inner[q] = inner[q] * rcp(inner[q] + gf[q])
        if q < count - 1:
            behind = ground_last[q] + up_inner[q] * gf[q]
            up_face[q + 1] = face[q + 1] * rcp(face[q + 1] + behind)
            gf[q + 1] = ground_first[q + 1] + up_face[q + 1] * behind
    down_inner, down_face, gl = [None] * count, [None] * (count + 1), [None] * count
    gl[count - 1] = ground_last[count - 1]
    for q in range(count - 1, -1, -1):
        down_inner[q] = inner[q] * rcp(inner[q] + gl[q])
        if q > 0:
            behind = ground_first[q] + down_inner[q] * gl[q]
            down_face[q] = face[q] * rcp(face[q] + behind)
            gl[q - 1] = ground_last[q - 1] + down_face[q] * behind
    zero = jnp.zeros_like(gf[0])

    def own(values):
        out = zero
        for q in range(count):
            if values[q] is not None:
                out = jnp.where(me == q, values[q], out)
        return out

    own_f, own_l, own_i = own(gf), own(gl), own(inner)
    scale = rcp(own_f * (own_l + own_i) + own_i * own_l)
    aa, bb, cc = (own_l + own_i) * scale, (own_f + own_i) * scale, own_i * scale
    from_low_f, from_low_l = [zero] * count, [zero] * count
    via_low = [zero] * count
    carry = zero
    for q in range(count - 2, -1, -1):
        via_low[q] = jnp.where(me == q + 1, 1.0, carry)
        from_low_l[q] = via_low[q] * up_face[q + 1]
        from_low_f[q] = from_low_l[q] * up_inner[q]
        carry = from_low_f[q]
    from_high_f, from_high_l = [zero] * count, [zero] * count
    via_high = [zero] * count
    carry = zero
    for q in range(1, count):
        via_high[q] = jnp.where(me == q - 1, 1.0, carry)
        from_high_f[q] = via_high[q] * down_face[q]
        from_high_l[q] = from_high_f[q] * down_inner[q]
        carry = from_high_l[q]
    return dict(
        aa=aa, bb=bb, cc=cc,
        low_f=from_low_f, low_l=from_low_l, high_f=from_high_f, high_l=from_high_l,
        via_low=via_low, via_high=via_high,
        up_inner=own(up_inner), up_face=own(up_face[1:]), down_inner=own(down_inner), down_face=own(down_face[:count]),
    )


def end_weights(ch, count, me, q):
    here = jnp.where(me == q, 1.0, 0.0)
    lf, ll = ch["low_f"][q] + here, ch["low_l"][q]
    hf, hl = ch["high_f"][q], ch["high_l"][q] + here
    return (
        ch["aa"] * lf + ch["cc"] * hf, ch["aa"] * ll + ch["cc"] * hl,
        ch["cc"] * lf + ch["bb"] * hf, ch["cc"] * ll + ch["bb"] * hl,
    )


def kernel(counts, t_hbm, c_hbm, out_ref, s):
    nx, ny, nz = counts
    mx, my, mz = lax.axis_index("gx"), lax.axis_index("gy"), lax.axis_index("gz")
    tc = s["tc"]
    load_c = pltpu.make_async_copy(c_hbm, tc.at[1], s["load"].at[1])
    load_t = pltpu.make_async_copy(t_hbm, tc.at[0], s["load"].at[0])
    load_c.start()
    load_t.start()
    barrier = pltpu.get_barrier_semaphore()
    greeted = 0
    for axis, me, count, reach in (("gx", mx, nx, 2), ("gz", mz, nz, 1), ("gy", my, ny, 1)):
        for step in reversed(near(count, reach)):
            pl.semaphore_signal(
                barrier, inc=1, device_id={axis: lax.rem(me + step, count)}, device_id_type=MESH
            )
            greeted += 1

    def put(name):
        def store(i, value):
            s[name][i] = value
        return store

    def load(name):
        return lambda i: s[name][i]

    halo_z = Halo("gz", nz, tc.at[:, pl.ds(0, NY)], tc.at[:, pl.ds((NZ - 1) * NY, NY)], s["hz"], s["hz_s"], s["hz_r"])
    halo_y = Halo("gy", ny, s["ey"].at[0], s["ey"].at[1], s["hy"], s["hy_s"], s["hy_r"])
    info_x = Gather("gx", nx, s["ix"], s["ix_s"], s["ix_r"])
    info_y = Gather("gy", ny, s["iy"], s["iy_s"], s["iy_r"])
    info_z = Gather("gz", nz, s["iz"], s["iz_s"], s["iz_r"])
    side_x = Gather("gx", nx, s["bx"], s["bx_s"], s["bx_r"])
    side_y = Gather("gy", ny, s["by"], s["by_s"], s["by_r"])
    side_z = Gather("gz", nz, s["bz"], s["bz_s"], s["bz_r"])
    relay_x = Relay("gx", nx, 2, s["rx"])
    relay_y = Relay("gy", ny, 1, s["ry"])
    relay_z = Relay("gz", nz, 1, s["rz"])

    load_c.wait()
    load_t.wait()
    for side, y in ((0, 0), (1, NY - 1)):
        for k in range(2):
            s["ey"][side, k] = tc[k, pl.ds(y, NZ, stride=NY), :]
    if greeted:
        pl.semaphore_wait(barrier, greeted)
    halo_z.start()
    halo_y.start()
    relay_x.fire(0)
    relay_y.fire(0)
    relay_z.fire(0)

    for half in range(2):
        for k, name in ((0, "tx"), (1, "cx")):
            block = jnp.concatenate(
                [tc[k, pl.ds(y, NZ, stride=NY), :] for y in range(16 * half, 16 * half + 16)], axis=0
            )
            s["ty" if k == 0 else "cy"][pl.ds(16 * half, 16)] = block.reshape(16, NZ, NX)
            s[name][half, pl.ds(0, NX), :] = block.T
            s[name][half, pl.ds(NX, 8), :] = jnp.ones((8, NX), jnp.float32)

    def cells(name, j):
        return jnp.stack([s[name][half, pl.ds(j, 8, stride=SEG), :] for half in range(2)])

    def put_cells(name, j, value):
        for half in range(2):
            s[name][half, pl.ds(j, 8, stride=SEG), :] = value[half]

    c = [cells("cx", j) for j in range(SEG + 1)]
    t = [cells("tx", j) for j in range(SEG + 1)]
    seg = lax.broadcasted_iota(jnp.int32, (2, 8, NX), 1)
    edges = [edge(c[j], c[j + 1]) for j in range(SEG)]
    flux = [2.0 * edges[j] * (t[j + 1] - t[j]) for j in range(SEG)]
    gap, gap_flux = edges.pop(), jnp.where(seg == 7, 0.0, flux[SEG - 1])
    flux[SEG - 1] = gap_flux
    before = pltpu.roll(gap_flux, 1, 1)
    for j in range(SEG):
        put_cells("fx", j, t[j] + 0.5 * (flux[j] - before))
        before = flux[j]
    one = jnp.ones_like(gap)
    g_first, g_last, inner = chain_matrix(
        edges, [one] * SEG, put("sx_rho"), put("sx_inv"), put("sx_p"), put("sx_q")
    )
    for k, value in enumerate((g_first, g_last, inner, gap)):
        s["l2"][k] = value.reshape(16, NX)

    def row(name, k, at):
        return s[name][k, pl.ds(at, 2, stride=8), :]

    grounds, edges = [], []
    for at in range(8):
        grounds += [row("l2", 0, at), row("l2", 1, at)]
        edges += [row("l2", 2, at)] + ([row("l2", 3, at)] if at < 7 else [])

    def put_node(name):
        def store(i, value):
            s[name][i % 2, pl.ds(i // 2, 2, stride=8), :] = value
        return store

    g_first, g_last, inner = chain_matrix(
        edges, grounds, put("l2_rho"), put("l2_inv"), put_node("l2_p"), put_node("l2_q")
    )
    for name, level in (("xp", "l2_p"), ("xq", "l2_q")):
        at_first, at_last = s[level][0].reshape(2, 8, NX), s[level][1].reshape(2, 8, NX)
        for j in range(SEG):
            put_cells(name, j, s["sx_p"][j] * at_first + s["sx_q"][j] * at_last)
    for k, name, x in ((0, "tx", 0), (1, "tx", NX - 1), (2, "cx", 0), (3, "cx", NX - 1)):
        for half in range(2):
            s["ix"][mx, pl.ds(half * 8 + k, 1), :] = s[name][half, pl.ds(x, 1), :]
    for k, value in ((4, g_first), (5, g_last), (6, inner)):
        s["ix"][mx, pl.ds(k, 2, stride=8), :] = value
    relay_x.wait(0)
    info_x.start()
    relay_y.wait(0)
    relay_y.fire(1)

    tz = [tc[0, pl.ds(z * NY, NY), :] for z in range(NZ)]
    cz = [tc[1, pl.ds(z * NY, NY), :] for z in range(NZ)]
    edges_z = [edge(cz[z], cz[z + 1]) for z in range(NZ - 1)]
    before = None
    for z in range(NZ):
        after = 2.0 * edges_z[z] * (tz[z + 1] - tz[z]) if z < NZ - 1 else None
        lap = after if before is None else (-before if after is None else after - before)
        before = after
        s["lz"][z] = lap
        if 0 < z < NZ - 1:
            for tile in range(NY // 8):
                s["lzy"][pl.ds(tile * 64 + z, 8, stride=8), :] = lap[tile * 8:tile * 8 + 8]
    edges_y = [edge(s["cy"][y], s["cy"][y + 1]) for y in range(NY - 1)]
    before = None
    for y in range(NY):
        after = 2.0 * edges_y[y] * (s["ty"][y + 1] - s["ty"][y]) if y < NY - 1 else None
        lap = after if before is None else (-before if after is None else after - before)
        before = after
        s["ly"][y] = lap
    one = jnp.ones((NZ, NX), jnp.float32)
    ends_y = chain_matrix(edges_y, [one] * NY, put("y_rho"), put("y_inv"), put("y_p"), put("y_q"))
    for k in range(3):
        s["iy"][my, k] = ends_y[k]
    one = jnp.ones((NY, NX), jnp.float32)
    ends_z = chain_matrix(edges_z, [one] * NZ, put("z_rho"), put("z_inv"), put("z_p"), put("z_q"))
    for k in range(3):
        s["iz"][mz, k] = ends_z[k]

    halo_y.wait_recv()
    halo_z.wait_recv()
    for side in range(2):
        at_wall = mz == (0, nz - 1)[side]
        z = (0, NZ - 1)[side]
        t_end, c_end = tc[0, pl.ds(z * NY, NY), :], tc[1, pl.ds(z * NY, NY), :]
        face = jnp.where(at_wall, c_end, edge(s["hz"][side, 1], c_end))
        beyond = jnp.where(at_wall, 0.0, s["hz"][side, 0])
        lap = s["lz"][z] + 2.0 * face * (beyond - t_end)
        s["lz"][z] = lap
        for tile in range(NY // 8):
            s["lzy"][pl.ds(tile * 64 + z, 8, stride=8), :] = lap[tile * 8:tile * 8 + 8]
        s["fz"][side] = face
    for side in range(2):
        at_wall = my == (0, ny - 1)[side]
        y = (0, NY - 1)[side]
        t_end, c_end = s["ty"][y], s["cy"][y]
        face = jnp.where(at_wall, c_end, edge(s["hy"][side, 1], c_end))
        beyond = jnp.where(at_wall, 0.0, s["hy"][side, 0])
        s["ly"][y] = s["ly"][y] + 2.0 * face * (beyond - t_end)
        s["fy"][side] = face

    for half in range(2):
        lap = s["ly"][pl.ds(16 * half, 16)].reshape(NX, NX) + s["lzy"][pl.ds(NX * half, NX), :]
        f = s["fx"][half] + lap.T
        s["fx"][half] = f
        for k, name in ((0, "xp"), (1, "xq")):
            part = jnp.sum((s[name][half] * f).reshape(16, 8, NX), axis=0)
            s["bx"][mx, pl.ds(2 * k + half, 1), :] = jnp.sum(part, axis=0, keepdims=True)
    side_x.start()

    relay_y.wait(1)
    relay_z.wait(0)
    face_low, face_high = s["fy"][0], s["fy"][1]
    s["iy"][my, 0] = s["iy"][my, 0] + jnp.where(my == 0, face_low, 0.0)
    s["iy"][my, 1] = s["iy"][my, 1] + jnp.where(my == ny - 1, face_high, 0.0)
    s["iy"][my, 3] = face_low
    info_y.start()
    face_low, face_high = s["fz"][0], s["fz"][1]
    s["iz"][mz, 0] = s["iz"][mz, 0] + jnp.where(mz == 0, face_low, 0.0)
    s["iz"][mz, 1] = s["iz"][mz, 1] + jnp.where(mz == nz - 1, face_high, 0.0)
    s["iz"][mz, 3] = face_low
    info_z.start()

    f = [cells("fx", j) for j in range(SEG)]
    s["l2_b"][0] = (f[0] + tree([s["sx_p"][j] * f[j] for j in range(1, SEG - 1)])).reshape(16, NX)
    s["l2_b"][1] = (f[SEG - 1] + tree([s["sx_q"][j] * f[j] for j in range(1, SEG - 1)])).reshape(16, NX)
    chain_base(16, lambda i: row("l2_b", i % 2, i // 2), load("l2_rho"), load("l2_inv"), put_node("l2_v"))
    nothing = jnp.zeros((2, NX), jnp.float32)
    put_node("l2_v")(0, nothing)
    put_node("l2_v")(15, nothing)
    at_first, at_last = s["l2_v"][0].reshape(2, 8, NX), s["l2_v"][1].reshape(2, 8, NX)

    def put_base(j, value):
        put_cells("xb", j, value + s["sx_p"][j] * at_first + s["sx_q"][j] * at_last)

    chain_base(SEG, lambda j: f[j], load("sx_rho"), load("sx_inv"), put_base)
    put_cells("xb", 0, at_first)
    put_cells("xb", SEG - 1, at_last)

    info_x.wait_recv()
    parts = [[row("ix", q, k) for k in range(7)] for q in range(nx)]
    faces = [None] * nx
    add_f, add_l = [None] * nx, [None] * nx
    gf, gl = [p[4] for p in parts], [p[5] for p in parts]
    add_f[0] = -parts[0][2] * parts[0][0]
    gf[0] = gf[0] + parts[0][2]
    add_l[nx - 1] = -parts[nx - 1][3] * parts[nx - 1][1]
    gl[nx - 1] = gl[nx - 1] + parts[nx - 1][3]
    for q in range(1, nx):
        faces[q] = edge(parts[q - 1][3], parts[q][2])
        flow = faces[q] * (parts[q][0] - parts[q - 1][1])
        add_f[q] = -flow
        add_l[q - 1] = flow
    ch = device_chain(nx, mx, gf, gl, [p[6] for p in parts], faces)
    const_f, const_l = 0.0, 0.0
    for q in range(nx):
        ff, fl, lf, ll = end_weights(ch, nx, mx, q)
        const_f = const_f + ff * add_f[q] + fl * add_l[q]
        const_l = const_l + lf * add_f[q] + ll * add_l[q]
        s["wx"][q, 0, pl.ds(0, 2), :] = ff
        s["wx"][q, 0, pl.ds(2, 2), :] = fl
        s["wx"][q, 1, pl.ds(0, 2), :] = lf
        s["wx"][q, 1, pl.ds(2, 2), :] = ll
    side_x.wait_recv()
    b = [s["bx"][q, pl.ds(0, 4), :] for q in range(nx)]
    first = tree([s["wx"][q, 0, pl.ds(0, 4), :] * b[q] for q in range(nx)])
    final = tree([s["wx"][q, 1, pl.ds(0, 4), :] * b[q] for q in range(nx)])
    first = first[0:2] + first[2:4] + const_f
    final = final[0:2] + final[2:4] + const_l

    sums_first, sums_last = [], []
    for half in range(2):
        u = s["xb"][half] + s["xp"][half] * first[half:half + 1] + s["xq"][half] * final[half:half + 1]
        rows = pl.ds(16 * half, 16)
        f = u.T.reshape(16, NZ, NX) - 0.5 * s["ly"][rows]
        s["fyy"][rows] = f
        sums_first += list(s["y_p"][rows] * f)
        sums_last += list(s["y_q"][rows] * f)
    s["by"][my, 0] = tree(sums_first)
    s["by"][my, 1] = tree(sums_last)
    side_y.start()

    chain_base(NY, load("fyy"), load("y_rho"), load("y_inv"), put("yb"))
    s["yb"][0] = jnp.zeros((NZ, NX), jnp.float32)
    s["yb"][NY - 1] = jnp.zeros((NZ, NX), jnp.float32)
    info_y.wait_recv()
    ch = device_chain(ny, my, *[[s["iy"][q, k] for q in range(ny)] for k in range(4)])
    for q in range(ny):
        for k, weight in enumerate(end_weights(ch, ny, my, q)):
            s["wy"][q, k] = weight
    info_z.wait_recv()
    ch = device_chain(nz, mz, *[[s["iz"][q, k] for q in range(nz)] for k in range(4)])
    for q in range(nz):
        s["wz"][q, 0] = ch["aa"] * ch["via_low"][q] + ch["cc"] * ch["via_high"][q]
        s["wz"][q, 1] = ch["cc"] * ch["via_low"][q] + ch["bb"] * ch["via_high"][q]
    for k, name in enumerate(("aa", "bb", "cc", "up_inner", "up_face", "down_inner", "down_face")):
        s["vz"][k] = ch[name]
    s["bz"][mz] = jnp.zeros((NY, NX), jnp.float32)
    side_y.wait_recv()
    first = tree([s["wy"][q, k] * s["by"][q, k] for q in range(ny) for k in range(2)])
    final = tree([s["wy"][q, 2 + k] * s["by"][q, k] for q in range(ny) for k in range(2)])
    for y in range(NY):
        s["u2"][pl.ds(y * 8, 8), :] = s["yb"][y] + s["y_p"][y] * first + s["y_q"][y] * final

    sums_first, sums_last = [], []
    for z in range(NZ):
        u = jnp.concatenate([s["u2"][pl.ds(tile * 64 + z, 8, stride=8), :] for tile in range(NY // 8)], axis=0)
        f = u - 0.5 * s["lz"][z]
        s["fzz"][z] = f
        sums_first.append(s["z_p"][z] * f)
        sums_last.append(s["z_q"][z] * f)
    sum_first, sum_last = tree(sums_first), tree(sums_last)
    s["bz_out"][0] = s["vz"][4] * (sum_last + s["vz"][3] * sum_first)
    s["bz_out"][1] = s["vz"][6] * (sum_first + s["vz"][5] * sum_last)

    def send_z(step):
        peer = lax.rem(mz + step, nz)
        return pltpu.make_async_remote_copy(
            src_ref=s["bz_out"].at[jnp.where(peer > mz, 0, 1)], dst_ref=s["bz"].at[mz],
            send_sem=side_z.send.at[step - 1], recv_sem=side_z.recv.at[mz],
            device_id={"gz": peer}, device_id_type=MESH,
        )

    for step in side_z.steps:
        send_z(step).start()
    first = s["vz"][0] * sum_first + s["vz"][2] * sum_last
    final = s["vz"][2] * sum_first + s["vz"][1] * sum_last
    chain_base(NZ, load("fzz"), load("z_rho"), load("z_inv"), put("zb"))
    s["zb"][0] = jnp.zeros((NY, NX), jnp.float32)
    s["zb"][NZ - 1] = jnp.zeros((NY, NX), jnp.float32)
    for group in (halo_y, halo_z, info_x, info_y, info_z, side_x, side_y):
        group.wait_send()
    side_z.wait_recv()
    first = first + tree([s["wz"][q, 0] * s["bz"][q] for q in range(nz)])
    final = final + tree([s["wz"][q, 1] * s["bz"][q] for q in range(nz)])
    for z in range(NZ):
        out_ref[pl.ds(z * NY, NY), :] = s["zb"][z] + s["z_p"][z] * first + s["z_q"][z] * final
    for step in side_z.steps:
        send_z(step).wait_send()


def scratch(counts):
    nx, ny, nz = counts
    f32 = jnp.float32
    ycells, zcells, xcells = (NY, NZ, NX), (NZ, NY, NX), (2, NX, NX)
    segs, nodes = (SEG, 2, 8, NX), (2, 16, NX)
    vmem = dict(
        tc=(2, NZ * NY, NX), ty=ycells, cy=ycells, tx=(2, NX + 8, NX), cx=(2, NX + 8, NX), fx=xcells, xp=xcells,
        xq=xcells, xb=xcells, sx_rho=segs, sx_inv=segs, sx_p=segs, sx_q=segs, l2=(4, 16, NX), l2_rho=(16, 2, NX),
        l2_inv=(16, 2, NX), l2_p=nodes, l2_q=nodes, l2_b=nodes, l2_v=nodes,
        fyy=ycells, ly=ycells, lz=zcells, fzz=zcells, lzy=(NZ * NY, NX), u2=(NZ * NY, NX),
        y_rho=ycells, y_inv=ycells, y_p=ycells, y_q=ycells, yb=ycells,
        z_rho=zcells, z_inv=zcells, z_p=zcells, z_q=zcells, zb=zcells,
        ey=(2, 2, NZ, NX), hy=(2, 2, NZ, NX), hz=(2, 2, NY, NX), fy=(2, NZ, NX), fz=(2, NY, NX),
        ix=(nx, 16, NX), bx=(nx, 8, NX), wx=(nx, 2, 8, NX),
        iy=(ny, 4, NZ, NX), by=(ny, 2, NZ, NX), wy=(ny, 4, NZ, NX),
        iz=(nz, 4, NY, NX), bz=(nz, NY, NX), bz_out=(2, NY, NX), wz=(nz, 2, NY, NX), vz=(7, NY, NX),
    )
    out = {name: pltpu.VMEM(shape, f32) for name, shape in vmem.items()}
    out["load"] = pltpu.SemaphoreType.DMA((2,))
    for name, count in (("hz", 2), ("hy", 2), ("ix", nx), ("iy", ny), ("iz", nz), ("bx", nx), ("by", ny), ("bz", nz)):
        out[name + "_s"] = pltpu.SemaphoreType.DMA((count,))
        out[name + "_r"] = pltpu.SemaphoreType.DMA((count,))
    for name in ("rx", "ry", "rz"):
        out[name] = pltpu.SemaphoreType.REGULAR((2,))
    return out


def solution(mesh):
    counts = (mesh.shape["gx"], mesh.shape["gy"], mesh.shape["gz"])
    shapes = scratch(counts)
    names = list(shapes)

    def body(t_hbm, c_hbm, out_ref, *refs):
        kernel(counts, t_hbm, c_hbm, out_ref, dict(zip(names, refs)))

    def on_device(thermal_state, diffusion_ratio):
        rows = NZ * NY
        out = pl.pallas_call(
            body,
            out_shape=jax.ShapeDtypeStruct((rows, NX), jnp.float32),
            in_specs=[pl.BlockSpec(memory_space=pltpu.HBM)] * 2,
            out_specs=pl.BlockSpec(memory_space=pltpu.VMEM),
            scratch_shapes=[shapes[name] for name in names],
            compiler_params=pltpu.CompilerParams(
                collective_id=0, has_side_effects=True, vmem_limit_bytes=24 * 1024 * 1024
            ),
        )(*[pltpu.with_memory_space_constraint(v.reshape(rows, NX), pltpu.HBM) for v in (thermal_state, diffusion_ratio)])
        return out.reshape(NZ, NY, NX)

    spec = P("gz", "gy", "gx")
    return jax.shard_map(on_device, mesh=mesh, in_specs=(spec, spec), out_specs=spec, check_vma=False)
```

time: 29.2 us -> 25.8 us (0.88)
  local copies, waits for them, and re-layouts: 2.47 us -> 0.66 us
  Pallas kernels: 26.6 us -> 25.1 us
    unnamed x5 -> x1, local copies, waits for them, and re-layouts: 2.47 us -> 0.66 us
    pallas_call x1, Pallas kernels: 26.6 us -> 25.1 us  [on_device(): pl.pallas_call(body, out_shape=jax.ShapeDtypeStruct((rows, NX), jnp.float...]
where the time goes in v2:
time: 25.8 us; the launch traced here: 25.7 us
  Pallas kernels  25.1 us (97%)
  local copies, waits for them, and re-layouts  0.66 us (3%)
    pallas_call x1, Pallas kernels, on_device(): pl.pallas_call(body, out_shape=jax.ShapeDtypeStruct((rows, NX), jnp.float...  25.1 us
    unnamed x1, local copies, waits for them, and re-layouts  0.66 us

profile of v2, /device:TPU:1, one launch (start us, length us, event | category | flops | bytes accessed | tf_op | source)
XLA Modules:
  0.0 25.7 jit_solution(17914953128564459045)
XLA Ops:
  0.0 25.1 %shard_map.28 = f32[256,128]{1,0:T(8,128)S(1)} custom-call(f32[256,128]{1,0:T(8,128)} %bitcast.4, f32[256,128]{1,0:T(8,128)} %bitcast.5), custom_call_target="tpu_custom_call" | custom-call | tf_op jit(solution)/shard_map/pallas_call | solution.py:567
  25.1 0.7 %copy.4 = f32[8,32,128]{2,1,0:T(8,128)} copy(f32[8,32,128]{2,1,0:T(8,128)S(1)} %bitcast.3) | data formatting | bytes 262144

commit v3 on v2

--- a/solution.py
+++ b/solution.py
@@ -26,28 +26,32 @@
         self.me = lax.axis_index(axis)
         self.steps = sorted(range(1, count), key=lambda step: -min(step, count - step))
 
-    def copy(self, slot, peer, step):
-        return pltpu.make_async_remote_copy(
-            src_ref=self.buf.at[slot],
-            dst_ref=self.buf.at[slot],
-            send_sem=self.send.at[step - 1],
-            recv_sem=self.recv.at[slot],
-            device_id={self.axis: peer},
-            device_id_type=MESH,
-        )
-
-    def start(self):
-        for step in self.steps:
-            self.copy(self.me, lax.rem(self.me + step, self.count), step).start()
-
-    def wait_recv(self):
+    def start(self, source=None):
         for step in self.steps:
             peer = lax.rem(self.me + step, self.count)
-            self.copy(peer, peer, step).wait_recv()
+            pltpu.make_async_remote_copy(
+                src_ref=self.buf.at[self.me] if source is None else source(peer),
+                dst_ref=self.buf.at[self.me],
+                send_sem=self.send,
+                recv_sem=self.recv,
+                device_id={self.axis: peer},
+                device_id_type=MESH,
+            ).start()
+
+    def all_peers(self):
+        slots = self.buf.at[pl.ds(0, self.count - 1)]
+        return pltpu.make_async_remote_copy(
+            src_ref=slots, dst_ref=slots, send_sem=self.send, recv_sem=self.recv,
+            device_id={self.axis: lax.rem(self.me + 1, self.count)}, device_id_type=MESH,
+        )
+
+    def wait_recv(self):
+        if self.count > 1:
+            self.all_peers().wait_recv()
 
     def wait_send(self):
-        for step in self.steps:
-            self.copy(self.me, lax.rem(self.me + step, self.count), step).wait_send()
+        if self.count > 1:
+            self.all_peers().wait_send()
 
 
 class Halo:
@@ -57,31 +61,31 @@
         self.ends = (high, low)
 
     def copy(self, side):
-        step = (1, self.count - 1)[side]
         return pltpu.make_async_remote_copy(
-            src_ref=self.ends[side],
-            dst_ref=self.buf.at[side],
-            send_sem=self.send.at[side],
-            recv_sem=self.recv.at[side],
-            device_id={self.axis: lax.rem(self.me + step, self.count)},
+            src_ref=self.buf if side is None else self.ends[side],
+            dst_ref=self.buf if side is None else self.buf.at[side],
+            send_sem=self.send,
+            recv_sem=self.recv,
+            device_id={self.axis: lax.rem(self.me + (self.count - 1 if side else 1), self.count)},
             device_id_type=MESH,
         )
 
     def start(self):
-        for side in range(2):
-            self.copy(side).start()
+        if self.count > 1:
+            for side in range(2):
+                self.copy(side).start()
 
     def wait_recv(self):
-        for side in range(2):
-            self.copy(side).wait_recv()
+        if self.count > 1:
+            self.copy(None).wait_recv()
 
     def wait_send(self):
-        for side in range(2):
-            self.copy(side).wait_send()
+        if self.count > 1:
+            self.copy(None).wait_send()
 
 
 def near(count, reach):
-    return sorted({s % count for r in range(1, reach + 1) for s in (r, -r)} - {0})
+    return sorted({s % count for r in range(1, reach + 1) for s in (r, -r)} - {0}, key=lambda s: min(s, count - s))
 
 
 class Relay:
@@ -233,8 +237,8 @@
     load_t.start()
     barrier = pltpu.get_barrier_semaphore()
     greeted = 0
-    for axis, me, count, reach in (("gx", mx, nx, 2), ("gz", mz, nz, 1), ("gy", my, ny, 1)):
-        for step in reversed(near(count, reach)):
+    for axis, me, count, reach in (("gz", mz, nz, 1), ("gy", my, ny, 1), ("gx", mx, nx, nx // 2)):
+        for step in near(count, reach):
             pl.semaphore_signal(
                 barrier, inc=1, device_id={axis: lax.rem(me + step, count)}, device_id_type=MESH
             )
@@ -256,7 +260,6 @@
     side_x = Gather("gx", nx, s["bx"], s["bx_s"], s["bx_r"])
     side_y = Gather("gy", ny, s["by"], s["by_s"], s["by_r"])
     side_z = Gather("gz", nz, s["bz"], s["bz_s"], s["bz_r"])
-    relay_x = Relay("gx", nx, 2, s["rx"])
     relay_y = Relay("gy", ny, 1, s["ry"])
     relay_z = Relay("gz", nz, 1, s["rz"])
 
@@ -269,7 +272,6 @@
         pl.semaphore_wait(barrier, greeted)
     halo_z.start()
     halo_y.start()
-    relay_x.fire(0)
     relay_y.fire(0)
     relay_z.fire(0)
 
@@ -332,10 +334,7 @@
             s["ix"][mx, pl.ds(half * 8 + k, 1), :] = s[name][half, pl.ds(x, 1), :]
     for k, value in ((4, g_first), (5, g_last), (6, inner)):
         s["ix"][mx, pl.ds(k, 2, stride=8), :] = value
-    relay_x.wait(0)
     info_x.start()
-    relay_y.wait(0)
-    relay_y.fire(1)
 
     tz = [tc[0, pl.ds(z * NY, NY), :] for z in range(NZ)]
     cz = [tc[1, pl.ds(z * NY, NY), :] for z in range(NZ)]
@@ -396,13 +395,9 @@
             s["bx"][mx, pl.ds(2 * k + half, 1), :] = jnp.sum(part, axis=0, keepdims=True)
     side_x.start()
 
-    relay_y.wait(1)
+    relay_y.wait(0)
+    relay_y.fire(1)
     relay_z.wait(0)
-    face_low, face_high = s["fy"][0], s["fy"][1]
-    s["iy"][my, 0] = s["iy"][my, 0] + jnp.where(my == 0, face_low, 0.0)
-    s["iy"][my, 1] = s["iy"][my, 1] + jnp.where(my == ny - 1, face_high, 0.0)
-    s["iy"][my, 3] = face_low
-    info_y.start()
     face_low, face_high = s["fz"][0], s["fz"][1]
     s["iz"][mz, 0] = s["iz"][mz, 0] + jnp.where(mz == 0, face_low, 0.0)
     s["iz"][mz, 1] = s["iz"][mz, 1] + jnp.where(mz == nz - 1, face_high, 0.0)
@@ -424,6 +419,13 @@
     chain_base(SEG, lambda j: f[j], load("sx_rho"), load("sx_inv"), put_base)
     put_cells("xb", 0, at_first)
     put_cells("xb", SEG - 1, at_last)
+
+    relay_y.wait(1)
+    face_low, face_high = s["fy"][0], s["fy"][1]
+    s["iy"][my, 0] = s["iy"][my, 0] + jnp.where(my == 0, face_low, 0.0)
+    s["iy"][my, 1] = s["iy"][my, 1] + jnp.where(my == ny - 1, face_high, 0.0)
+    s["iy"][my, 3] = face_low
+    info_y.start()
 
     info_x.wait_recv()
     parts = [[row("ix", q, k) for k in range(7)] for q in range(nx)]
@@ -501,16 +503,7 @@
     s["bz_out"][0] = s["vz"][4] * (sum_last + s["vz"][3] * sum_first)
     s["bz_out"][1] = s["vz"][6] * (sum_first + s["vz"][5] * sum_last)
 
-    def send_z(step):
-        peer = lax.rem(mz + step, nz)
-        return pltpu.make_async_remote_copy(
-            src_ref=s["bz_out"].at[jnp.where(peer > mz, 0, 1)], dst_ref=s["bz"].at[mz],
-            send_sem=side_z.send.at[step - 1], recv_sem=side_z.recv.at[mz],
-            device_id={"gz": peer}, device_id_type=MESH,
-        )
-
-    for step in side_z.steps:
-        send_z(step).start()
+    side_z.start(lambda peer: s["bz_out"].at[jnp.where(peer > mz, 0, 1)])
     first = s["vz"][0] * sum_first + s["vz"][2] * sum_last
     final = s["vz"][2] * sum_first + s["vz"][1] * sum_last
     chain_base(NZ, load("fzz"), load("z_rho"), load("z_inv"), put("zb"))
@@ -523,8 +516,7 @@
     final = final + tree([s["wz"][q, 1] * s["bz"][q] for q in range(nz)])
     for z in range(NZ):
         out_ref[pl.ds(z * NY, NY), :] = s["zb"][z] + s["z_p"][z] * first + s["z_q"][z] * final
-    for step in side_z.steps:
-        send_z(step).wait_send()
+    side_z.wait_send()
 
 
 def scratch(counts):
@@ -546,10 +538,10 @@
     )
     out = {name: pltpu.VMEM(shape, f32) for name, shape in vmem.items()}
     out["load"] = pltpu.SemaphoreType.DMA((2,))
-    for name, count in (("hz", 2), ("hy", 2), ("ix", nx), ("iy", ny), ("iz", nz), ("bx", nx), ("by", ny), ("bz", nz)):
-        out[name + "_s"] = pltpu.SemaphoreType.DMA((count,))
-        out[name + "_r"] = pltpu.SemaphoreType.DMA((count,))
-    for name in ("rx", "ry", "rz"):
+    for name in ("hz", "hy", "ix", "iy", "iz", "bx", "by", "bz"):
+        out[name + "_s"] = pltpu.SemaphoreType.DMA
+        out[name + "_r"] = pltpu.SemaphoreType.DMA
+    for name in ("ry", "rz"):
         out[name] = pltpu.SemaphoreType.REGULAR((2,))
     return out
 

time: 25.8 us -> 25.2 us (0.977)
  Pallas kernels: 25.1 us -> 24.5 us
    pallas_call x1, Pallas kernels: 25.1 us -> 24.5 us  [on_device(): pl.pallas_call(body, out_shape=jax.ShapeDtypeStruct((rows, NX), jnp.float...]
where the time goes in v3:
time: 25.2 us; the launch traced here: 25.1 us
  Pallas kernels  24.5 us (97%)
  local copies, waits for them, and re-layouts  0.66 us (3%)
    pallas_call x1, Pallas kernels, on_device(): pl.pallas_call(body, out_shape=jax.ShapeDtypeStruct((rows, NX), jnp.float...  24.5 us
    unnamed x1, local copies, waits for them, and re-layouts  0.66 us

profile of v3, /device:TPU:1, one launch (start us, length us, event | category | flops | bytes accessed | tf_op | source)
XLA Modules:
  0.0 25.1 jit_solution(12313879679437210410)
XLA Ops:
  0.0 24.5 %shard_map.28 = f32[256,128]{1,0:T(8,128)S(1)} custom-call(f32[256,128]{1,0:T(8,128)} %bitcast.4, f32[256,128]{1,0:T(8,128)} %bitcast.5), custom_call_target="tpu_custom_call" | custom-call | tf_op jit(solution)/shard_map/pallas_call | solution.py:559
  24.5 0.7 %copy.4 = f32[8,32,128]{2,1,0:T(8,128)} copy(f32[8,32,128]{2,1,0:T(8,128)S(1)} %bitcast.3) | data formatting | bytes 262144
